TPU v7x, 32 devices: a whole 2x2x4 slice. The times are simulated.
32 devices in a mesh: dp: 8 (over z, y), tensor: 4 (over x, core).
Axes of the slice: x: 2, y: 2, z: 4, core: 2. Of those that a mesh axis runs over, the one named last changes fastest.
Arguments:
- tokens_in: float32 [8192, 768], P('dp'), may hold values from -6 to 6
- cotangent: float32 [8192, 768], P('dp')
- segment_ids: int32 [8192], P('dp'), may hold values from -1 to 59, as said below
- long_seq: int32 [8], P('dp'), may hold values from 0 to 1
- weights: float32 [2, 192, 4, 9216], P(None, 'dp', 'tensor')
- left_stats: float32 [2, 192, 4, 9216], P(None, 'dp', 'tensor')
- right_stats: float32 [2, 192, 4, 9216], P(None, 'dp', 'tensor')
- left_roots: float32 [2, 192, 4, 9216], P(None, 'dp', 'tensor')
- right_roots: float32 [2, 192, 4, 9216], P(None, 'dp', 'tensor')
- split_params: float32 [2, 4, 1152], P(None, 'tensor', 'dp'), may hold values from -1 to 1
- shared_params: float32 [2, 6, 768], P(None, None, 'dp')
Outputs:
- block_out: float32 [8192, 768], P('dp')
- input_grad: float32 [8192, 768], P('dp')
- weight_grads: float32 [2, 192, 4, 9216], P(None, 'dp', 'tensor')
- new_weights: float32 [2, 192, 4, 9216], P(None, 'dp', 'tensor')
- new_left_stats: float32 [2, 192, 4, 9216], P(None, 'dp', 'tensor')
- new_right_stats: float32 [2, 192, 4, 9216], P(None, 'dp', 'tensor')
- split_grads: float32 [2, 4, 1152], P(None, 'tensor', 'dp')
- new_split_params: float32 [2, 4, 1152], P(None, 'tensor', 'dp')
- shared_grads: float32 [2, 6, 768], P(None, None, 'dp')
- new_shared_params: float32 [2, 6, 768], P(None, None, 'dp')
- grad_norm: float32 [], replicated
Inputs may be any that keep to these rules, and one draw needn't show every extreme that they name: `segment_ids`: within each sequence (1024 slots on indices of dp whose long_seq is 1, 256 otherwise, laid end to end) the ids start at 0, never fall and rise by at most one from a slot to the next; padding (-1) fills only the sequence's last slots, at most a quarter of them.
All inputs are finite; a program needn't handle non-finite values.
Results may differ from a plain program's by a relative error of at most 0.035.
Values may be sent and summed in bfloat16 or wider, within the bound.
A program may use at most 192 MiB of HBM per device.

v0:
```python
import math

import jax
import jax.numpy as jnp
from jax import lax
from jax.sharding import PartitionSpec as P

D = 768
HEADS = 12
FF = 3072
HD = 64
B = 96
LAYERS = 2
SEQ_SHORT = 256
SEQ_LONG = 1024


clip_limit = 100.0
rate_matrix = 0.06
rate_vector = 0.2
decay = 0.5
eps_norm = 1e-06
eps_layer = 1e-06
big_negative = -1e30
highest = lax.Precision.HIGHEST


def layer_norm(hidden, gain_vec, shift_vec):
    row_mean = jnp.mean(hidden, axis=-1, keepdims=True)
    centered = hidden - row_mean
    row_var = jnp.mean(centered * centered, axis=-1, keepdims=True)
    return centered * lax.rsqrt(row_var + eps_layer) * gain_vec + shift_vec


def gelu_exact(values):
    return jax.nn.gelu(values, approximate=False)


def matmul_low(left_mat, right_mat):
    return jnp.dot(left_mat, right_mat, preferred_element_type=jnp.float32)


def inner_rows(left_mat, right_mat):
    return lax.dot_general(
        left_mat, right_mat, (((0,), (0,)), ((), ())), preferred_element_type=jnp.float32
    )


def times_trans(left_mat, right_mat):
    return lax.dot_general(
        left_mat, right_mat, (((1,), (1,)), ((), ())), preferred_element_type=jnp.float32
    )


def unpack_layer(blocks, embed_dev, inner_dev):
    row_groups = blocks.shape[0]
    block_size = blocks.shape[2]
    qkv_count = 3 * embed_dev // block_size
    up_count = inner_dev // block_size
    out_count = embed_dev // block_size

    def by_rows(part_blocks):
        block_count = part_blocks.shape[1]
        return jnp.transpose(part_blocks, (0, 2, 1, 3)).reshape(
            row_groups * block_size, block_count * block_size
        )

    def by_cols(part_blocks):
        block_count = part_blocks.shape[1]
        return jnp.transpose(part_blocks, (1, 2, 0, 3)).reshape(
            block_count * block_size, row_groups * block_size
        )

    qkv_weight = by_rows(blocks[:, :qkv_count])
    up_weight = by_rows(blocks[:, qkv_count : qkv_count + up_count])
    out_weight = by_cols(blocks[:, qkv_count + up_count : qkv_count + up_count + out_count])
    down_weight = by_cols(blocks[:, qkv_count + up_count + out_count :])
    return (qkv_weight, out_weight, up_weight, down_weight)


def pack_layer(qkv_grad, out_grad, up_grad, down_grad, block_size):
    row_groups = qkv_grad.shape[0] // block_size

    def from_rows(matrix):
        block_count = matrix.shape[1] // block_size
        return jnp.transpose(
            matrix.reshape(row_groups, block_size, block_count, block_size), (0, 2, 1, 3)
        )

    def from_cols(matrix):
        block_count = matrix.shape[0] // block_size
        return jnp.transpose(
            matrix.reshape(block_count, block_size, row_groups, block_size), (2, 0, 1, 3)
        )

    return jnp.concatenate(
        [from_rows(qkv_grad), from_rows(up_grad), from_cols(out_grad), from_cols(down_grad)], axis=1
    )


def masked_scores(query_block, key_window, query_seq, key_seq, query_seg, key_seg, score_scale):
    scores = (
        jnp.einsum("qhd,khd->hqk", query_block, key_window, preferred_element_type=jnp.float32)
        * score_scale
    )
    allowed = (query_seq[:, None] == key_seq[None, :]) & (query_seg[:, None] == key_seg[None, :])
    return jnp.where(allowed[None], scores, big_negative)


def attention_forward(queries, keys_all, values_all, seq_index, segments, block_rows, score_scale):
    block_count = queries.shape[0] // block_rows

    def one_block(block_index):
        row_start = block_index * block_rows
        query_block = lax.dynamic_slice_in_dim(queries, row_start, block_rows, 0)
        scores = masked_scores(
            query_block,
            keys_all,
            lax.dynamic_slice_in_dim(seq_index, row_start, block_rows, 0),
            seq_index,
            lax.dynamic_slice_in_dim(segments, row_start, block_rows, 0),
            segments,
            score_scale,
        )
        row_max = jnp.max(scores, axis=-1, keepdims=True)
        exponent = jnp.exp(scores - row_max)
        row_total = jnp.sum(exponent, axis=-1, keepdims=True)
        attn_probs = (exponent / row_total).astype(jnp.bfloat16)
        attended = jnp.einsum(
            "hqk,khd->qhd", attn_probs, values_all, preferred_element_type=jnp.float32
        )
        return (attended, (row_max + jnp.log(row_total))[..., 0])

    return lax.map(one_block, jnp.arange(block_count, dtype=jnp.int32))


def attention_backward(
    queries, keys_all, values_all, grad_out, log_total, seq_index, segments, block_rows, score_scale
):
    token_count = queries.shape[0]
    block_count = token_count // block_rows
    zero_grad = jnp.zeros(keys_all.shape, jnp.float32)

    def one_block(carry_pair, block_index):
        key_grad, value_grad = carry_pair
        row_start = block_index * block_rows
        query_block = lax.dynamic_slice_in_dim(queries, row_start, block_rows, 0)
        out_block = lax.dynamic_slice_in_dim(grad_out, row_start, block_rows, 0)
        scores = masked_scores(
            query_block,
            keys_all,
            lax.dynamic_slice_in_dim(seq_index, row_start, block_rows, 0),
            seq_index,
            lax.dynamic_slice_in_dim(segments, row_start, block_rows, 0),
            segments,
            score_scale,
        )
        lse_block = lax.dynamic_index_in_dim(log_total, block_index, 0, keepdims=False)
        attn_probs = jnp.exp(scores - lse_block[..., None])
        prob_grad = jnp.einsum(
            "qhd,khd->hqk", out_block, values_all, preferred_element_type=jnp.float32
        )
        row_delta = jnp.sum(attn_probs * prob_grad, axis=-1, keepdims=True)
        score_grad = (attn_probs * (prob_grad - row_delta)).astype(jnp.bfloat16)
        query_grad = (
            jnp.einsum("hqk,khd->qhd", score_grad, keys_all, preferred_element_type=jnp.float32)
            * score_scale
        )
        key_part = (
            jnp.einsum("hqk,qhd->khd", score_grad, query_block, preferred_element_type=jnp.float32)
            * score_scale
        )
        value_part = jnp.einsum(
            "hqk,qhd->khd",
            attn_probs.astype(jnp.bfloat16),
            out_block,
            preferred_element_type=jnp.float32,
        )
        key_grad = key_grad + key_part
        value_grad = value_grad + value_part
        return ((key_grad, value_grad), query_grad)

    (key_grad, value_grad), query_grad = lax.scan(
        one_block, (zero_grad, zero_grad), jnp.arange(block_count, dtype=jnp.int32)
    )
    return (query_grad.reshape(keys_all.shape), key_grad, value_grad)


def body(
    tokens_in,
    cotangent,
    segment_ids,
    long_seq,
    weights,
    left_stats,
    right_stats,
    left_roots,
    right_roots,
    split_params,
    shared_params,
):
    full_weights, full_split, full_shared = (
        lax.all_gather(weights, "dp", axis=1, tiled=True),
        lax.all_gather(split_params, "dp", axis=2, tiled=True),
        lax.all_gather(shared_params, "dp", axis=2, tiled=True),
    )
    tensor_count = lax.axis_size("tensor")
    embed_dev = D // tensor_count
    inner_dev = FF // tensor_count
    heads_local = HEADS // tensor_count
    token_count = tokens_in.shape[0]
    window = SEQ_LONG
    block_rows = min(512, window)
    score_scale = 1.0 / math.sqrt(HD)
    seq_length = jnp.where(long_seq[0] > 0, SEQ_LONG, SEQ_SHORT)
    positions = jnp.arange(token_count, dtype=jnp.int32)
    seq_index = positions // seq_length
    valid_rows = (segment_ids >= 0).astype(jnp.float32)
    matrices = []
    for layer_index in range(LAYERS):
        blocks = full_weights[layer_index, :, 0].astype(jnp.bfloat16).reshape(D // B, -1, B, B)
        matrices.append(unpack_layer(blocks, embed_dev, inner_dev))
    hidden_state = tokens_in
    kept_state = []
    for layer_index in range(LAYERS):
        qkv_weight, out_weight, up_weight, down_weight = matrices[layer_index]
        shared = full_shared[layer_index]
        bias_table = full_split[layer_index, 0].reshape(embed_dev, 6)
        up_bias = bias_table[:, 2:].reshape(inner_dev)
        normed = layer_norm(hidden_state, shared[0], shared[1]).astype(jnp.bfloat16)
        qkv_bias = jnp.concatenate(
            [bias_table[:, 0], jnp.zeros((embed_dev,), jnp.float32), bias_table[:, 1]]
        )
        projected = (matmul_low(normed, qkv_weight) + qkv_bias).astype(jnp.bfloat16)
        queries = projected[:, :embed_dev].reshape(token_count, heads_local, HD)
        keys_all = projected[:, embed_dev : 2 * embed_dev].reshape(token_count, heads_local, HD)
        values_all = projected[:, 2 * embed_dev :].reshape(token_count, heads_local, HD)
        attended, log_total = attention_forward(
            queries, keys_all, values_all, seq_index, segment_ids, block_rows, score_scale
        )
        attended = attended.reshape(token_count, embed_dev).astype(jnp.bfloat16)
        attn_branch = lax.psum(
            matmul_low(attended, out_weight).astype(jnp.bfloat16), "tensor"
        ).astype(jnp.float32)
        middle = hidden_state + attn_branch + shared[4]
        normed_mid = layer_norm(middle, shared[2], shared[3]).astype(jnp.bfloat16)
        pre_act = matmul_low(normed_mid, up_weight) + up_bias
        activation = gelu_exact(pre_act).astype(jnp.bfloat16)
        mlp_branch = lax.psum(
            matmul_low(activation, down_weight).astype(jnp.bfloat16), "tensor"
        ).astype(jnp.float32)
        kept_state.append(
            (
                hidden_state,
                normed,
                queries,
                keys_all,
                values_all,
                attended,
                log_total,
                middle,
                normed_mid,
                pre_act,
                activation,
            )
        )
        hidden_state = middle + mlp_branch + shared[5]
    grad_state = cotangent * valid_rows[:, None]
    layer_grads = [None] * LAYERS
    for layer_index in reversed(range(LAYERS)):
        (
            hidden_in,
            normed,
            queries,
            keys_all,
            values_all,
            attended,
            log_total,
            middle,
            normed_mid,
            pre_act,
            activation,
        ) = kept_state[layer_index]
        qkv_weight, out_weight, up_weight, down_weight = matrices[layer_index]
        shared = full_shared[layer_index]
        down_bias_grad = jnp.sum(grad_state, axis=0)
        grad_low = grad_state.astype(jnp.bfloat16)
        down_grad = inner_rows(activation, grad_low)
        act_grad = times_trans(grad_low, down_weight)
        gelu_pull = jax.vjp(gelu_exact, pre_act)[1]
        pre_grad = gelu_pull(act_grad)[0].astype(jnp.bfloat16)
        up_bias_grad = jnp.sum(pre_grad, axis=0, dtype=jnp.float32)
        up_grad = inner_rows(normed_mid, pre_grad)
        normed_mid_grad = lax.psum(times_trans(pre_grad, up_weight), "tensor")
        norm_pull = jax.vjp(layer_norm, middle, shared[2], shared[3])[1]
        middle_ln, gain_two_grad, shift_two_grad = norm_pull(normed_mid_grad)
        middle_grad = grad_state + middle_ln
        out_bias_grad = jnp.sum(middle_grad, axis=0)
        middle_low = middle_grad.astype(jnp.bfloat16)
        out_grad = inner_rows(attended, middle_low)
        attended_grad = (
            times_trans(middle_low, out_weight)
            .astype(jnp.bfloat16)
            .reshape(token_count, heads_local, HD)
        )
        query_grad, key_grad, value_grad = attention_backward(
            queries,
            keys_all,
            values_all,
            attended_grad,
            log_total,
            seq_index,
            segment_ids,
            block_rows,
            score_scale,
        )
        proj_grad = jnp.concatenate(
            [
                query_grad.reshape(token_count, embed_dev),
                key_grad.reshape(token_count, embed_dev),
                value_grad.reshape(token_count, embed_dev),
            ],
            axis=1,
        ).astype(jnp.bfloat16)
        query_bias_grad = jnp.sum(proj_grad[:, :embed_dev], axis=0, dtype=jnp.float32)
        value_bias_grad = jnp.sum(proj_grad[:, 2 * embed_dev :], axis=0, dtype=jnp.float32)
        qkv_grad = inner_rows(normed, proj_grad)
        normed_grad = lax.psum(times_trans(proj_grad, qkv_weight), "tensor")
        input_pull = jax.vjp(layer_norm, hidden_in, shared[0], shared[1])[1]
        hidden_ln, gain_one_grad, shift_one_grad = input_pull(normed_grad)
        grad_state = middle_grad + hidden_ln
        block_grads = pack_layer(qkv_grad, out_grad, up_grad, down_grad, B).reshape(-1, 1, B * B)
        split_vec = jnp.concatenate(
            [
                query_bias_grad[:, None],
                value_bias_grad[:, None],
                up_bias_grad.reshape(embed_dev, 4),
            ],
            axis=1,
        ).reshape(1, -1)
        shared_vec = jnp.stack(
            [
                gain_one_grad,
                shift_one_grad,
                gain_two_grad,
                shift_two_grad,
                out_bias_grad,
                down_bias_grad,
            ]
        )
        layer_grads[layer_index] = (block_grads, split_vec, shared_vec)
    weight_grad, split_grad, shared_grad = (
        lax.psum_scatter(
            jnp.stack([entry[0] for entry in layer_grads]), "dp", scatter_dimension=1, tiled=True
        ),
        lax.psum_scatter(
            jnp.stack([entry[1] for entry in layer_grads]), "dp", scatter_dimension=2, tiled=True
        ),
        lax.psum_scatter(
            jnp.stack([entry[2] for entry in layer_grads]), "dp", scatter_dimension=2, tiled=True
        ),
    )
    dp_index = lax.axis_index("dp")
    lead_shard = (lax.axis_index("tensor") == 0).astype(jnp.float32)
    slice_len = split_grad.shape[-1]
    global_pos = dp_index * slice_len + jnp.arange(slice_len, dtype=jnp.int32)
    table_column = global_pos % 6
    segment_of = (table_column >= 1).astype(jnp.int32) + (table_column >= 2).astype(jnp.int32)
    selector = (segment_of[:, None] == jnp.arange(3, dtype=jnp.int32)[None, :]).astype(jnp.float32)
    split_sq = split_grad[:, 0] * split_grad[:, 0]
    split_rows = jnp.dot(split_sq, selector, precision=highest)
    shared_sq = shared_grad * shared_grad
    shared_rows = jnp.sum(shared_sq, axis=-1) * lead_shard
    local_total = (
        jnp.sum(weight_grad * weight_grad) + jnp.sum(split_sq) + lead_shard * jnp.sum(shared_sq)
    )
    total_sq, split_rows, shared_rows = lax.psum(
        (local_total, split_rows, shared_rows), ("dp", "tensor")
    )
    grad_norm = jnp.sqrt(total_sq)
    factor = clip_limit / jnp.maximum(grad_norm, clip_limit)
    squared = factor * factor
    block_shape = weight_grad.shape[:-1] + (B, B)
    left_mats = left_roots.reshape(block_shape)
    right_mats = right_roots.reshape(block_shape)
    clipped = weight_grad * factor
    clipped_mats = clipped.reshape(block_shape)
    new_left = decay * left_stats + (1.0 - decay) * jnp.einsum(
        "...ij,...kj->...ik", clipped_mats, clipped_mats, precision=highest
    ).reshape(left_stats.shape)
    new_right = decay * right_stats + (1.0 - decay) * jnp.einsum(
        "...ji,...jk->...ik", clipped_mats, clipped_mats, precision=highest
    ).reshape(right_stats.shape)
    partial_dir = jnp.einsum("...ij,...jk->...ik", left_mats, clipped_mats, precision=highest)
    direction = jnp.einsum("...ij,...jk->...ik", partial_dir, right_mats, precision=highest)
    mean_sq = jnp.mean(direction * direction, axis=(-2, -1), keepdims=True)
    step_mats = direction * lax.rsqrt(mean_sq + eps_norm)
    new_weights = weights - rate_matrix * step_mats.reshape(weights.shape)
    vector_sizes = jnp.array([D, D, FF], jnp.float32)
    split_mean = jnp.dot(split_rows / vector_sizes[None, :], selector.T, precision=highest)
    split_clip = split_grad * factor
    new_split = split_params - rate_vector * split_clip * lax.rsqrt(
        squared * split_mean[:, None, :] + eps_norm
    )
    shared_clip = shared_grad * factor
    shared_mean = shared_rows / D
    new_shared = shared_params - rate_vector * shared_clip * lax.rsqrt(
        squared * shared_mean[..., None] + eps_norm
    )
    return (
        hidden_state,
        grad_state,
        clipped,
        new_weights,
        new_left,
        new_right,
        split_clip,
        new_split,
        shared_clip,
        new_shared,
        grad_norm,
    )


def solution(mesh):
    in_specs = (
        P("dp", None),
        P("dp", None),
        P("dp"),
        P("dp"),
        P(None, "dp", "tensor", None),
        P(None, "dp", "tensor", None),
        P(None, "dp", "tensor", None),
        P(None, "dp", "tensor", None),
        P(None, "dp", "tensor", None),
        P(None, "tensor", "dp"),
        P(None, None, "dp"),
    )
    out_specs = (
        P("dp", None),
        P("dp", None),
        P(None, "dp", "tensor", None),
        P(None, "dp", "tensor", None),
        P(None, "dp", "tensor", None),
        P(None, "dp", "tensor", None),
        P(None, "tensor", "dp"),
        P(None, "tensor", "dp"),
        P(None, None, "dp"),
        P(None, None, "dp"),
        P(),
    )
    return jax.shard_map(body, mesh=mesh, in_specs=in_specs, out_specs=out_specs, check_vma=False)
```

profile of v0, /device:TPU:0, one launch (start us, length us, event | category | flops | bytes accessed | tf_op | source)
XLA Modules:
  0.0 1677.5 jit_solution(12675870928453135307)
XLA Ops:
  11.7 34.9 %all_gather.11 = f32[2,1,1152]{0,1,2:T(1,128)S(1)} all-gather(f32[2,1,144]{0,1,2:T(1,128)S(1)} %copy.170), channel_id=1, replica_groups=mesh['dp'=8,'tensor'=4] {'dp'}, dimensions={2}, use_global_device_ids=true | all-gather | bytes 10368 | tf_op jit(solution)/shard_map/all_gather | solution.py:204
  46.6 18.9 %slice_reduce_fusion.2 = (f32[1152]{0:T(1024)S(1)}, f32[1152]{0:T(1024)S(1)}) fusion(f32[2,1,1152]{0,1,2:T(1,128)S(1)} %all_gather.11), kind=kLoop, calls=%fused_computation.205 | loop fusion | bytes 18432 | tf_op jit(solution)/shard_map/slice | solution.py:228
  66.6 34.5 %all_gather.9 = f32[2,6,768]{1,0,2:T(2,128)S(1)} all-gather(f32[2,6,96]{1,0,2:T(2,128)S(1)} %copy.168), channel_id=1, replica_groups=mesh['dp'=8,'tensor'=4] {'dp'}, dimensions={2}, use_global_device_ids=true | all-gather | bytes 41472 | tf_op jit(solution)/shard_map/all_gather | solution.py:205
  102.7 33.8 %slice_reduce_fusion.4 = (f32[768]{0:T(1024)}, f32[768]{0:T(1024)}, f32[768]{0:T(1024)}, f32[768]{0:T(1024)}, f32[768]{0:T(1024)}, /*index=5*/f32[768]{0:T(1024)...) fusion(f32[2,6,768]{1,0,2:T(2,128)S(1)} %all_gather.9), kind=kLoop, calls=%fused_computation.211 | loop fusion | bytes 73728 | tf_op jit(solution)/shard_map/slice | solution.py:267
  138.2 80.9 %all-gather.2.cloned.1.call-done = bf16[2,192,1,9216]{3,2,1,0:T(2,128)(2,1)} async-done(((bf16[2,24,1,9216]{3,2,1,0:T(2,128)(2,1)}), bf16[2,192,1,9216]{3,2,1,0:T(2,128)(2,1)}) %all-gather.2.cloned.1.call-update) | async-done | bytes 7077904 | tf_op jit(solution)/shard_map/all_gather | solution.py:203
  219.1 45.8 %slice_reduce_fusion = (bf16[192,9216]{1,0:T(8,128)(2,1)}, bf16[192,9216]{1,0:T(8,128)(2,1)}) fusion(bf16[2,192,1,9216]{3,2,1,0:T(2,128)(2,1)} %all-gather.2.cloned.1.call-done), kind=kLoop, calls=%fused_computation.89 | loop fusion | bytes 14155776 | tf_op jit(solution)/shard_map/slice | solution.py:221
  264.9 7.8 convert_element_type.156
  287.9 20.4 %while.54 = (s32[]{:T(128)}, bf16[2,512,3,64]{1,3,2,0:T(8,128)(2,1)}, f32[2,3,512]{2,1,0:T(4,128)}, s32[2]{0:T(128)}, s32[1024]{0:T(1024)S(1)}, /*index=5*/s32[1...) while((s32[]{:T(128)}, ...), condition=%wide.region_5.6_spmd, body=%wide.region_2.5_spmd.sunk | while | flops 423098880 | bytes 23993568 | solution.py:134
  334.9 24.3 %all-reduce.12.cloned.1.call-done = bf16[1024,768]{1,0:T(8,128)(2,1)} async-done(((bf16[1024,768]{1,0:T(8,128)(2,1)}), bf16[1024,768]{1,0:T(8,128)(2,1)}) %all-reduce.12.cloned.1.call-update) | async-done | bytes 1572880 | tf_op jit(solution)/shard_map/psum | solution.py:242
  363.3 9.7 multiply_convert_fusion.3
  376.9 6.0 convert_element_type.167
  388.2 31.7 %all-reduce.14.cloned.1.call-done = bf16[1024,768]{1,0:T(8,128)(2,1)} async-done(((bf16[1024,768]{1,0:T(8,128)(2,1)}), bf16[1024,768]{1,0:T(8,128)(2,1)}) %all-reduce.14.cloned.1.call-update) | async-done | bytes 1572880 | tf_op jit(solution)/shard_map/psum | solution.py:249
  428.6 18.9 %while.55 = (s32[]{:T(128)}, bf16[2,512,3,64]{1,3,2,0:T(8,128)(2,1)}, f32[2,3,512]{2,1,0:T(4,128)}, s32[2]{0:T(128)S(1)}, s32[1024]{0:T(1024)S(1)}, /*index=5*/s...) while((s32[]{:T(128)}, ...), condition=%wide.region_15.16_spmd, body=%wide.region_12.15_spmd.sunk | while | flops 423098880 | bytes 23993568 | solution.py:134
  461.4 4.2 reshape.678
  473.0 22.5 %all-reduce.16.cloned.1.call-done = bf16[1024,768]{1,0:T(8,128)(2,1)} async-done(((bf16[1024,768]{1,0:T(8,128)(2,1)}), bf16[1024,768]{1,0:T(8,128)(2,1)}) %all-reduce.16.cloned.1.call-update) | async-done | bytes 1572880 | tf_op jit(solution)/shard_map/psum | solution.py:242
  499.6 9.4 multiply_convert_fusion.2
  516.6 4.4 convolution_convert_fusion
  521.1 64.1 %all-reduce.20.cloned.1.call-done = f32[1024,768]{1,0:T(8,128)} async-done(((f32[1024,768]{1,0:T(8,128)}), f32[1024,768]{1,0:T(8,128)}) %all-reduce.20.cloned.1.call-update) | async-done | bytes 3145744 | tf_op jit(solution)/shard_map/psum | solution.py:294
  589.4 41.5 %all-reduce.18.cloned.1.call-done = bf16[1024,768]{1,0:T(8,128)(2,1)} async-done(((bf16[1024,768]{1,0:T(8,128)(2,1)}), bf16[1024,768]{1,0:T(8,128)(2,1)}) %all-reduce.18.cloned.1.call-update) | async-done | bytes 1572880 | tf_op jit(solution)/shard_map/psum | solution.py:249
  630.9 4.6 fusion.134
  640.0 51.2 %while.56 = (s32[]{:T(128)}, f32[1024,3,64]{0,2,1:T(8,128)}, f32[1024,3,64]{0,2,1:T(8,128)}, bf16[2,512,3,64]{1,3,2,0:T(8,128)(2,1)}, s32[2]{0:T(128)S(1)}, /*in...) while((s32[]{:T(128)}, f32[1024,3,64]{0,2,1:T(8,128)}, ...), condition=%wide.region_25.26_spmd.clone, body=%wide.region_23.25_spmd.clone.sunk | while | flops 1032878592 | bytes 107807872 | solution.py:183
  642.0 4.8 fusion.254
  649.4 4.7 multiply_reduce_fusion.22
  667.3 4.8 fusion.254
  674.7 4.7 multiply_reduce_fusion.22
  701.4 4.6 fusion.145
  705.9 4.6 reshape.690
  710.5 4.3 fusion.126
  714.8 4.4 reshape.691
  719.3 5.6 copy.253
  727.2 40.6 %all-reduce.22.cloned.1.call-done = f32[1024,768]{1,0:T(8,128)} async-done(((f32[1024,768]{1,0:T(8,128)}), f32[1024,768]{1,0:T(8,128)}) %all-reduce.22.cloned.1.call-update) | async-done | bytes 3145744 | tf_op jit(solution)/shard_map/psum | solution.py:328
  792.1 4.5 copy.189
  799.1 4.6 fusion.144
  803.7 4.4 reshape.687
  808.2 5.3 fusion.96
  813.5 4.4 reshape.688
  817.9 5.4 copy.254
  825.8 27.9 %all-reduce.24.cloned.1.call-done = f32[1024,768]{1,0:T(8,128)} async-done(((f32[1024,768]{1,0:T(8,128)}), f32[1024,768]{1,0:T(8,128)}) %all-reduce.24.cloned.1.call-update) | async-done | bytes 3145744 | tf_op jit(solution)/shard_map/psum | solution.py:294
  863.4 51.5 %while.57 = (s32[]{:T(128)}, f32[1024,3,64]{0,2,1:T(8,128)}, f32[1024,3,64]{0,2,1:T(8,128)}, bf16[2,512,3,64]{1,3,2,0:T(8,128)(2,1)}, s32[2]{0:T(128)S(1)}, /*in...) while((s32[]{:T(128)}, f32[1024,3,64]{0,2,1:T(8,128)}, ...), condition=%wide.region_34.35_spmd.clone, body=%wide.region_32.34_spmd.clone.sunk | while | flops 1032878592 | bytes 107807872 | solution.py:183
  865.6 4.8 fusion.267
  873.0 4.7 multiply_reduce_fusion.23
  890.9 4.8 fusion.267
  898.4 4.7 multiply_reduce_fusion.23
  910.7 4.2 fusion.269
  927.2 4.3 pad_maximum_fusion.2
  931.6 5.3 copy.191
  937.0 13.5 stack_reshape.13
  958.1 4.5 copy.184
  962.6 29.1 %all-reduce.26.cloned.1.call-done = f32[1024,768]{1,0:T(8,128)} async-done(((f32[1024,768]{1,0:T(8,128)}), f32[1024,768]{1,0:T(8,128)}) %all-reduce.26.cloned.1.call-update) | async-done | bytes 3145744 | tf_op jit(solution)/shard_map/psum | solution.py:328
  1005.8 6.1 pad_maximum_fusion.1
  1013.7 9.1 copy.186
  1022.8 13.3 stack_reshape.12
  1036.1 16.8 pad_maximum_fusion
  1054.4 4.2 reduce.23
  1061.1 4.2 reduce.24
  1068.4 54.0 %reduce-scatter.9.cloned.1.call-done = f32[96,12]{1,0:T(8,128)} async-done(((f32[768,12]{1,0:T(8,128)}), f32[96,12]{1,0:T(8,128)}) %reduce-scatter.9.cloned.1.call-update) | async-done | bytes 4624
  1124.7 438.4 %all-reduce.28.cloned.1.call-done = f32[2,192,1,9216]{3,0,2,1:T(2,128)} async-done(((f32[2,192,1,9216]{3,0,2,1:T(2,128)}), f32[2,192,1,9216]{3,0,2,1:T(2,128)}) %all-reduce.28.cloned.1.call-update) | async-done | bytes 14155792
  1570.8 39.3 %all-reduce.1 = (f32[]{:T(128)}, f32[2,3]{1,0:T(2,128)S(1)}, f32[2,6]{1,0:T(2,128)S(1)}) all-reduce(f32[]{:T(128)S(6)} %add.406, f32[2,3]{1,0:T(2,128)S(1)} %fusion.107, f32[2,6]{1,0:T(2,128)S(1)} %broadcast_multiply_fusion.6), channel_id=1, replica_groups=mesh['dp'=8,'tensor'=4] {'dp','tensor'}, use_global_device_ids=true, to_apply=%region_62.63 | all-reduce | flops 19 | bytes 152 | tf_op jit(solution)/shard_map/psum | solution.py:377
  1616.9 5.3 fusion.84
  1622.3 6.4 fusion.86
  1634.4 4.5 fusion.88
  1646.0 5.0 sub.124
  1651.0 5.1 reshape.712
  1659.8 5.7 add_multiply_fusion
  (651 shorter events, 326.0 us)
Async XLA Ops:
  7.2 59.2 %copy-start.8 = (f32[1024,768]{1,0:T(8,128)S(1)}, f32[1024,768]{1,0:T(8,128)}, u32[]{:S(2)}) copy-start(f32[1024,768]{1,0:T(8,128)} %param.20) | copy-start | bytes 9437188
  7.2 211.9 %all-gather.2.cloned.1.call-start = ((), (), s32[]{:S(2)}) async-start(), calls=%async_computation.2 | async-start | bytes 15925248 | tf_op jit(solution)/shard_map/all_gather | solution.py:203
  11.3 347.9 %all-reduce.12.cloned.1.call-start = ((), (), s32[]{:S(2)}) async-start(), calls=%async_computation.3 | async-start | bytes 3145728 | tf_op jit(solution)/shard_map/psum | solution.py:242
  65.6 37.1 %copy-start.60 = (f32[192,6]{1,0:T(8,128)}, f32[192,6]{1,0:T(8,128)S(1)}, u32[]{:S(2)}) copy-start(f32[192,6]{1,0:T(8,128)S(1)} %reshape_squeeze.6) | copy-start | bytes 13828
  65.8 36.9 %copy-start.59 = (f32[192,6]{1,0:T(8,128)}, f32[192,6]{1,0:T(8,128)S(1)}, u32[]{:S(2)}) copy-start(f32[192,6]{1,0:T(8,128)S(1)} %reshape_squeeze.7) | copy-start | bytes 13828
  102.2 34.3 %copy-start.81 = (f32[1024]{0:T(1024)}, f32[1024]{0:T(1024)S(1)}, u32[]{:S(2)}) copy-start(f32[1024]{0:T(1024)S(1)} %broadcast_multiply_fusion.4) | copy-start | bytes 12292
  102.7 35.5 %copy-start.102 = (f32[1024]{0:T(1024)}, f32[1024]{0:T(1024)S(1)}, u32[]{:S(2)}) copy-start(f32[1024]{0:T(1024)S(1)} %multiply_reduce_fusion.13) | copy-start | bytes 12292
  102.7 35.5 %copy-start.90 = (f32[1024]{0:T(1024)}, f32[1024]{0:T(1024)S(1)}, u32[]{:S(2)}) copy-start(f32[1024]{0:T(1024)S(1)} %fusion.113) | copy-start | bytes 12292
  136.5 128.4 %copy-start.86 = (f32[768]{0:T(1024)}, f32[768]{0:T(1024)S(1)}, u32[]{:S(2)}) copy-start(f32[768]{0:T(1024)S(1)} %get-tuple-element.403) | copy-start | bytes 9220
  136.5 225.2 %copy-start.98 = (f32[768]{0:T(1024)}, f32[768]{0:T(1024)S(1)}, u32[]{:S(2)}) copy-start(f32[768]{0:T(1024)S(1)} %get-tuple-element.400) | copy-start | bytes 9220
  136.5 286.8 %copy-start.88 = (f32[768]{0:T(1024)}, f32[768]{0:T(1024)S(1)}, u32[]{:S(2)}) copy-start(f32[768]{0:T(1024)S(1)} %get-tuple-element.397) | copy-start | bytes 9220
  317.6 102.3 %all-reduce.14.cloned.1.call-start = ((), (), s32[]{:S(2)}) async-start(), calls=%async_computation.4 | async-start | bytes 3145728 | tf_op jit(solution)/shard_map/psum | solution.py:249
  318.7 43.0 %copy-start.141 = (f32[768]{0:T(1024)}, f32[768]{0:T(1024)S(1)}, u32[]{:S(2)}) copy-start(f32[768]{0:T(1024)S(1)} %add.373) | copy-start | bytes 9220
  327.5 31.7 %copy-start.117 = (f32[768]{0:T(1024)S(1)}, f32[768]{0:T(1024)}, u32[]{:S(2)}) copy-start(f32[768]{0:T(1024)} %get-tuple-element.401) | copy-start | bytes 9220
  361.2 11.9 copy-start.12
  361.2 11.9 copy-start.92
  361.7 11.4 copy-start.104
  361.7 11.4 copy-start.100
  363.3 10.9 copy-start.68
  376.9 118.7 %all-reduce.16.cloned.1.call-start = ((), (), s32[]{:S(2)}) async-start(), calls=%async_computation.5 | async-start | bytes 3145728 | tf_op jit(solution)/shard_map/psum | solution.py:242
  384.2 35.7 %copy-start.116 = (f32[768]{0:T(1024)S(1)}, f32[768]{0:T(1024)}, u32[]{:S(2)}) copy-start(f32[768]{0:T(1024)} %get-tuple-element.398) | copy-start | bytes 9220
  422.8 72.8 %copy-start.6 = (f32[1024,768]{1,0:T(8,128)}, f32[1024,768]{1,0:T(8,128)S(1)}, u32[]{:S(2)}) copy-start(f32[1024,768]{1,0:T(8,128)S(1)} %get-tuple-element.520) | copy-start | bytes 9437188
  452.4 132.7 %all-reduce.20.cloned.1.call-start = ((), (), s32[]{:S(2)}) async-start(), calls=%async_computation.7 | async-start | bytes 6291456 | tf_op jit(solution)/shard_map/psum | solution.py:294
  465.6 29.9 %copy-start.114 = (f32[768]{0:T(1024)S(1)}, f32[768]{0:T(1024)}, u32[]{:S(2)}) copy-start(f32[768]{0:T(1024)} %get-tuple-element.395) | copy-start | bytes 9220
  497.4 11.6 copy-start.14
  497.5 133.5 %copy-start.96 = (f32[1024]{0:T(1024)}, f32[1024]{0:T(1024)S(1)}, u32[]{:S(2)}) copy-start(f32[1024]{0:T(1024)S(1)} %broadcast_multiply_fusion.1) | copy-start | bytes 12292
  498.0 11.0 copy-start.110
  516.5 114.4 %all-reduce.18.cloned.1.call-start = ((), (), s32[]{:S(2)}) async-start(), calls=%async_computation.6 | async-start | bytes 3145728 | tf_op jit(solution)/shard_map/psum | solution.py:249
  516.5 68.6 %copy-start.15 = (f32[1024,768]{1,0:T(8,128)S(1)}, f32[1024,768]{1,0:T(8,128)}, u32[]{:S(2)}) copy-start(f32[1024,768]{1,0:T(8,128)} %copy-done.14) | copy-start | bytes 9437188
  521.0 246.8 %all-reduce.22.cloned.1.call-start = ((), (), s32[]{:S(2)}) async-start(), calls=%async_computation.8 | async-start | bytes 6291456 | tf_op jit(solution)/shard_map/psum | solution.py:328
  640.0 9.4 copy-start.43
  665.3 9.4 copy-start.43
  699.2 154.6 %all-reduce.24.cloned.1.call-start = ((), (), s32[]{:S(2)}) async-start(), calls=%async_computation.9 | async-start | bytes 6291456 | tf_op jit(solution)/shard_map/psum | solution.py:294
  719.3 48.6 %copy-start.7 = (f32[1024,768]{1,0:T(8,128)S(1)}, f32[1024,768]{1,0:T(8,128)}, u32[]{:S(2)}) copy-start(f32[1024,768]{1,0:T(8,128)} %copy-done.6) | copy-start | bytes 9437188
  719.3 48.6 %copy-start.84 = (f32[1024]{0:T(1024)S(1)}, f32[1024]{0:T(1024)}, u32[]{:S(2)}) copy-start(f32[1024]{0:T(1024)} %copy-done.83) | copy-start | bytes 12292
  719.3 48.6 %copy-start.89 = (f32[768]{0:T(1024)S(1)}, f32[768]{0:T(1024)}, u32[]{:S(2)}) copy-start(f32[768]{0:T(1024)} %copy-done.88) | copy-start | bytes 9220
  785.1 206.7 %all-reduce.26.cloned.1.call-start = ((), (), s32[]{:S(2)}) async-start(), calls=%async_computation.10 | async-start | bytes 6291456 | tf_op jit(solution)/shard_map/psum | solution.py:328
  825.8 31.5 %copy-start.105 = (f32[1024]{0:T(1024)S(1)}, f32[1024]{0:T(1024)}, u32[]{:S(2)}) copy-start(f32[1024]{0:T(1024)} %copy-done.104) | copy-start | bytes 12292
  863.6 9.4 copy-start.41
  889.0 9.4 copy-start.41
  923.0 143.6 %reduce-scatter.7.cloned.1.call-start = ((), (), s32[]{:S(2)}) async-start(), calls=%async_computation.11 | async-start | bytes 663552
  936.9 13.6 copy-start.131
  936.9 13.6 copy-start.132
  936.9 13.6 copy-start.133
  936.9 13.6 copy-start.134
  936.9 13.6 copy-start.135
  936.9 13.6 copy-start.136
  936.9 14.2 copy-start.122
  936.9 14.2 copy-start.121
  936.9 14.2 copy-start.120
  936.9 14.3 copy-start.58
  936.9 14.5 copy-start.64
  936.9 14.8 copy-start.75
  937.0 15.0 copy-start.113
  937.0 16.2 copy-start.80
  958.1 33.7 %copy-start.9 = (f32[1024,768]{1,0:T(8,128)S(1)}, f32[1024,768]{1,0:T(8,128)}, u32[]{:S(2)}) copy-start(f32[1024,768]{1,0:T(8,128)} %param.20) | copy-start | bytes 9437188
  958.1 33.7 %copy-start.82 = (f32[1024]{0:T(1024)S(1)}, f32[1024]{0:T(1024)}, u32[]{:S(2)}) copy-start(f32[1024]{0:T(1024)} %copy-done.81) | copy-start | bytes 12292
  958.1 33.7 %copy-start.87 = (f32[768]{0:T(1024)S(1)}, f32[768]{0:T(1024)}, u32[]{:S(2)}) copy-start(f32[768]{0:T(1024)} %copy-done.86) | copy-start | bytes 9220
  958.1 33.7 %copy-start.91 = (f32[1024]{0:T(1024)S(1)}, f32[1024]{0:T(1024)}, u32[]{:S(2)}) copy-start(f32[1024]{0:T(1024)} %copy-done.90) | copy-start | bytes 12292
  962.6 32.9 %copy-start.103 = (f32[1024]{0:T(1024)S(1)}, f32[1024]{0:T(1024)}, u32[]{:S(2)}) copy-start(f32[1024]{0:T(1024)} %copy-done.102) | copy-start | bytes 12292
  962.6 159.9 %reduce-scatter.9.cloned.1.call-start = ((), (), s32[]{:S(2)}) async-start(), calls=%async_computation.12 | async-start | bytes 442368
  1036.1 527.0 %all-reduce.28.cloned.1.call-start = ((), (), s32[]{:S(2)}) async-start(), calls=%async_computation.13 | async-start | bytes 28311552
  1622.3 11.3 copy-start.146
  1622.3 11.3 copy-start.152
  (134 other events, 510.8 us)
Sparse Core Ops, SparseCore 0:
  11.5 207.6 all-gather.1
  317.7 41.5 all-reduce.11
  377.0 42.8 all-reduce.13
  452.6 42.9 all-reduce.15
  516.6 68.4 all-reduce.19
  587.9 42.9 all-reduce.17
  699.3 68.4 all-reduce.21
  785.2 68.5 all-reduce.23
  923.1 68.5 all-reduce.25
  995.4 62.2 reduce-scatter.6
  1061.9 60.4 reduce-scatter.8
  1126.9 436.1 all-reduce.27
where the time goes:
time: 1690 us; the launch traced here: 1680 us
  waiting for transfers between devices  855 us (51%)
  local copies, waits for them, and re-layouts  345 us (20%)
  matrix products  196 us (12%)
  other arithmetic  136 us (8%)
  blocking collectives  109 us (6%)
  between operations  21.6 us (1%)
    unnamed x15, waiting for transfers between devices  493 us
    psum x2, waiting for transfers between devices, body(): normed_mid_grad = lax.psum(times_trans(pre_grad, up_weight), 'tensor')  92 us
    all_gather x1, waiting for transfers between devices, body(): lax.all_gather(weights, 'dp', axis=1, tiled=True)  80.9 us
    psum x2, waiting for transfers between devices, body(): lax.psum(matmul_low(activation, down_weight).astype(jnp.bfloat16), 'tensor')  73.2 us
    psum x2, waiting for transfers between devices, body(): normed_grad = lax.psum(times_trans(proj_grad, qkv_weight), 'tensor')  69.7 us
    unnamed x306, local copies, waits for them, and re-layouts  49.1 us
    psum x2, waiting for transfers between devices, body(): lax.psum(matmul_low(attended, out_weight).astype(jnp.bfloat16), 'tensor')  46.8 us
    slice x1, local copies, waits for them, and re-layouts, body(): full_weights[layer_index, :, 0].astype(jnp.bfloat16)  45.8 us
  transfers between devices with their start and end apart: 12, of which 11 were waited for; matrix products, arithmetic and copies ran while one was open for 18% of the time, Pallas kernels for 0%

commit v1 on v0

--- a/solution.py
+++ b/solution.py
@@ -1,8 +1,11 @@
+import functools
 import math
 
 import jax
 import jax.numpy as jnp
 from jax import lax
+from jax.experimental import pallas as pl
+from jax.experimental.pallas import tpu as pltpu
 from jax.sharding import PartitionSpec as P
 
 D = 768
@@ -422,6 +425,1174 @@
     )
 
 
+F32 = jnp.float32
+BF16 = jnp.bfloat16
+MESH = pl.DeviceIdType.MESH
+CHUNKS = 4
+HALF = 128
+CHUNK = 2 * HALF
+ROWS = CHUNKS * CHUNK
+HEADS_DEV = 3
+GROUPS = D // B
+GROUP = 24
+PARTS = ((0, 1, 2, 3, 4, 5, 14, 15), tuple(range(6, 14)), tuple(range(16, 24)))
+TRANSPOSED = (frozenset((14, 15)), frozenset(), frozenset(range(16, 24)))
+
+
+def dot_nn(left_mat, right_mat):
+    return lax.dot_general(left_mat, right_mat, (((1,), (0,)), ((), ())), preferred_element_type=F32)
+
+
+def dot_nt(left_mat, right_mat):
+    return lax.dot_general(left_mat, right_mat, (((1,), (1,)), ((), ())), preferred_element_type=F32)
+
+
+def dot_tn(left_mat, right_mat):
+    return lax.dot_general(left_mat, right_mat, (((0,), (0,)), ((), ())), preferred_element_type=F32)
+
+
+def lanes_of(shape):
+    return lax.broadcasted_iota(jnp.int32, shape, len(shape) - 1)
+
+
+def norm_rows(rows):
+    mean = jnp.mean(rows, axis=-1, keepdims=True)
+    centered = rows - mean
+    var = jnp.mean(centered * centered, axis=-1, keepdims=True)
+    inv = lax.rsqrt(var + eps_layer)
+    return centered * inv, inv
+
+
+def norm_back(grad, rows, gain):
+    hat, inv = norm_rows(rows)
+    scaled = grad * gain
+    mean_one = jnp.mean(scaled, axis=-1, keepdims=True)
+    mean_two = jnp.mean(scaled * hat, axis=-1, keepdims=True)
+    d_rows = inv * (scaled - mean_one - hat * mean_two)
+    return d_rows, jnp.sum(grad * hat, axis=0, keepdims=True), jnp.sum(grad, axis=0, keepdims=True)
+
+
+def table_selector(shape):
+    row = lax.broadcasted_iota(jnp.int32, shape, 0)
+    col = lax.broadcasted_iota(jnp.int32, shape, 1)
+    up_row = 6 * (col >> 2) + 2 + (col & 3)
+    hit = (col < B) & (row == up_row)
+    hit = hit | ((col >= 128) & (col < 152) & (row == 6 * (col - 128)))
+    hit = hit | ((col >= 152) & (col < 176) & (row == 6 * (col - 152) + 1))
+    return hit.astype(F32)
+
+
+def flat_to_square(x_zero, x_one, x_two, place):
+    lane = lanes_of((24, 128))
+    place[pl.ds(0, 24, stride=4), :] = x_zero
+    place[pl.ds(1, 24, stride=4), :] = jnp.where(
+        lane < 32, pltpu.roll(x_zero, 32, 1), pltpu.roll(x_one, 32, 1)
+    )
+    place[pl.ds(2, 24, stride=4), :] = jnp.where(
+        lane < 64, pltpu.roll(x_one, 64, 1), pltpu.roll(x_two, 64, 1)
+    )
+    place[pl.ds(3, 24, stride=4), :] = pltpu.roll(x_two, 96, 1)
+    return place[...][:, :B]
+
+
+def square_to_flat(square, place):
+    lane = lanes_of((24, 128))
+    place[:, 0:B] = square
+    m_zero, m_one, m_two, m_three = [place[pl.ds(m, 24, stride=4), :] for m in range(4)]
+    one_back = pltpu.roll(m_one, 96, 1)
+    two_back = pltpu.roll(m_two, 64, 1)
+    return (
+        jnp.where(lane < 96, m_zero, one_back),
+        jnp.where(lane < 64, one_back, two_back),
+        jnp.where(lane < 32, two_back, pltpu.roll(m_three, 32, 1)),
+    )
+
+
+def train_kernel(
+    n_y,
+    x_hbm,
+    ct_hbm,
+    seg_ref,
+    long_ref,
+    w_hbm,
+    split_ref,
+    shared_ref,
+    bo_hbm,
+    ig_hbm,
+    gb_hbm,
+    sg_ref,
+    nm_ref,
+    wt,
+    a_all,
+    c_all,
+    q_all,
+    k_all,
+    v_all,
+    v_tr,
+    o_all,
+    lse_all,
+    z_all,
+    gp_all,
+    res,
+    y_own,
+    y_all,
+    g_all,
+    du_all,
+    dx_all,
+    dk_acc,
+    dv_acc,
+    stage,
+    core_in,
+    x_in,
+    dw,
+    rs_one,
+    rs_two,
+    place,
+    g_out,
+    x_out,
+    kid_col,
+    kid_row,
+    vecs,
+    bias_row,
+    gvecs,
+    gbias,
+    sib_in,
+    msg_in,
+    gmsg_in,
+    gmsg_out,
+    nb_out,
+    nb_in,
+    nd_in,
+    g_s,
+    g_r,
+    c_s,
+    c_r,
+    x_s,
+    x_r,
+    a_s,
+    a_r,
+    p_s,
+    p_r,
+    t_s,
+    t_r,
+    load_sem,
+    land_sem,
+    ct_sem,
+    out_sem,
+    far_s,
+    far_r,
+    gout_sem,
+    m_s,
+    m_r,
+    gm_s,
+    gm_r,
+    sib_s,
+    sib_r,
+    nb_s,
+    nb_r,
+    nd_s,
+    nd_r,
+):
+    n_dp = GROUPS
+    n_z = n_dp // n_y
+    me = lax.axis_index("dp")
+    ten = lax.axis_index("tensor")
+    my_z, my_y = me // n_y, lax.rem(me, n_y)
+    my_x, my_c = ten // 2, lax.rem(ten, 2)
+    other_c = 1 - my_c
+    sibling = (me, 2 * my_x + other_c)
+    across = (me, 2 * (1 - my_x) + my_c)
+    scale = 1.0 / math.sqrt(HD)
+
+    def dp_dev(index):
+        return (index, ten)
+
+    def z_peer(step):
+        return lax.rem(my_z + step, n_z)
+
+    def remote(src, dst, send, recv, dev):
+        return pltpu.make_async_remote_copy(
+            src_ref=src, dst_ref=dst, send_sem=send, recv_sem=recv, device_id=dev, device_id_type=MESH
+        )
+
+    def load_rows(j, which):
+        half = my_c if which == 0 else other_c
+        return pltpu.make_async_copy(x_hbm.at[j, half], res.at[which, j], load_sem.at[which, j])
+
+    def load_blocks(l):
+        return pltpu.make_async_copy(
+            w_hbm.at[l], g_out.at[l, :, pl.ds(0, 72)], land_sem.at[l]
+        )
+
+    for l in range(LAYERS):
+        load_blocks(l).start()
+    for j in range(CHUNKS):
+        load_rows(j, 0).start()
+        load_rows(j, 1).start()
+
+    barrier = pltpu.get_barrier_semaphore()
+    for step in range(1, n_dp):
+        pl.semaphore_signal(
+            barrier, inc=1, device_id=dp_dev(lax.rem(me + step, n_dp)), device_id_type=MESH
+        )
+    pl.semaphore_signal(barrier, inc=1, device_id=sibling, device_id_type=MESH)
+    pl.semaphore_signal(barrier, inc=1, device_id=across, device_id_type=MESH)
+
+    sel = table_selector((144, 256))
+    for l in range(LAYERS):
+        row = lax.dot_general(
+            jnp.broadcast_to(split_ref[l : l + 1, :], (8, 144)),
+            sel,
+            (((1,), (0,)), ((), ())),
+            precision=highest,
+            preferred_element_type=F32,
+        )
+        msg_in[me, 8 * l : 8 * l + 8, :] = row
+        msg_in[me, 8 * l : 8 * l + 6, 0:B] = shared_ref[6 * l : 6 * l + 6, :]
+
+    pl.semaphore_wait(barrier, n_dp + 1)
+
+    def msg_copy(step):
+        return remote(
+            msg_in.at[me], msg_in.at[me], m_s.at[step - 1], m_r.at[me],
+            dp_dev(lax.rem(me + step, n_dp)),
+        )
+
+    def msg_from(step):
+        src = lax.rem(me + step, n_dp)
+        return remote(msg_in.at[src], msg_in.at[src], m_s.at[step - 1], m_r.at[src], dp_dev(src))
+
+    for step in range(1, n_dp):
+        msg_copy(step).start()
+
+    def gather_send(l, p, slab, k, dev):
+        return remote(
+            wt.at[l, p, slab], wt.at[l, p, slab], g_s.at[l, p, k], g_r.at[l, p, slab], dp_dev(dev)
+        )
+
+    def y_peers():
+        return [my_z * n_y + lax.rem(my_y + s, n_y) for s in range(1, n_y)]
+
+    def gather_begin(l, p):
+        for s in range(1, n_z):
+            gather_send(l, p, me, s - 1, z_peer(s) * n_y + my_y).start()
+        gather_send(l, p, me, n_z - 1, y_peers()[0]).start()
+
+    def gather_forward(l, p):
+        for s in range(1, n_z):
+            slab = z_peer(s) * n_y + my_y
+            gather_send(l, p, slab, n_z + s - 1, slab).wait_recv()
+            gather_send(l, p, slab, n_z + s - 1, y_peers()[0]).start()
+
+    def gather_finish(l, p):
+        for s in range(0, n_z):
+            slab = z_peer(s) * n_y + lax.rem(my_y + 1, n_y)
+            gather_send(l, p, slab, 0, slab).wait_recv()
+
+    def gather_drain(l, p):
+        for k in range(2 * n_z - 1):
+            gather_send(l, p, me, k, me).wait_send()
+
+    def relayout(l, p):
+        cols = []
+        for b in range(8):
+            blk = PARTS[p][b]
+            xs = [g_out[l, blk, pl.ds(m, 24, stride=3), :] for m in range(3)]
+            square = flat_to_square(*xs, place.at[b])
+            cols.append(jnp.transpose(square) if blk in TRANSPOSED[p] else square)
+        wt[l, p, me] = jnp.concatenate(cols, axis=1).astype(BF16)
+
+    def relayout_layer(l, carry):
+        load_blocks(l).wait()
+        for p in range(3):
+            relayout(l, p)
+            gather_begin(l, p)
+        return carry
+
+    lax.fori_loop(0, LAYERS, relayout_layer, 0)
+
+    seq_shift = jnp.where(long_ref[0, 0] > 0, 0, 1)
+    seg = seg_ref[...]
+    pos = lax.broadcasted_iota(jnp.int32, (8, 128), 0) * 128 + lax.broadcasted_iota(
+        jnp.int32, (8, 128), 1
+    )
+    seq = (pos >> 8) * seq_shift
+    kid = jnp.where(seg >= 0, seq * 64 + seg, -1 - seq).astype(F32)
+    for r in range(8):
+        kid_row[r // 2, 0:1, 128 * (r % 2) : 128 * (r % 2) + 128] = kid[r : r + 1, :]
+        kid_col[r] = jnp.transpose(
+            jnp.broadcast_to(kid[r : r + 1, :], (128, 128))
+        )
+
+    gvecs[...] = jnp.zeros_like(gvecs)
+    gbias[...] = jnp.zeros_like(gbias)
+
+    for step in range(1, n_dp):
+        msg_from(step).wait_recv()
+    for l in range(LAYERS):
+        vecs[l] = jnp.concatenate(
+            [msg_in[s, 8 * l : 8 * l + 8, 0:B] for s in range(n_dp)], axis=1
+        )
+        rows = [msg_in[s, 8 * l : 8 * l + 8, 128:256] for s in range(n_dp)]
+        pad = jnp.zeros((8, D // 4), F32)
+        bias_row[l] = jnp.concatenate(
+            [r[:, 0:24] for r in rows]
+            + [pad]
+            + [r[:, 24:48] for r in rows]
+            + [jnp.zeros((8, 64), F32)],
+            axis=1,
+        )
+
+    low_half = lanes_of((CHUNK, 128)) < 64
+
+    def vec(l, k):
+        return vecs[l, k : k + 1, :]
+
+    def core_copy(j):
+        return remote(stage.at[j, other_c], core_in.at[j], c_s.at[j], c_r.at[j], sibling)
+
+    def x_copy(j, par):
+        return remote(stage.at[j, my_c], x_in.at[par, j], x_s.at[par, j], x_r.at[par, j], across)
+
+    def own_copy(ref, j):
+        return remote(ref.at[j, my_c], ref.at[j, my_c], a_s.at[j], a_r.at[j], sibling)
+
+    def send_partial(j, value):
+        stage[j] = value.astype(BF16).reshape(2, HALF, D)
+        core_copy(j).start()
+
+    def pass_on(j, par):
+        core_copy(j).wait()
+        mine = stage[j, my_c].astype(F32) + core_in[j].astype(F32)
+        stage[j, my_c] = mine.astype(BF16)
+        x_copy(j, par).start()
+
+    def total(j, par):
+        x_copy(j, par).wait()
+        return stage[j, my_c].astype(F32) + x_in[par, j].astype(F32)
+
+    def project(l, j):
+        rows = a_all[l, j].reshape(CHUNK, D)
+        weight = wt[l, 0].reshape(D, D)[:, 0:640]
+        out = dot_nn(rows, weight) + bias_row[l, 0:1, :]
+        tiles = [out[:, 128 * t : 128 * t + 128] for t in range(5)]
+        q_roll = pltpu.roll(tiles[0], 64, 1)
+        v_roll = pltpu.roll(tiles[3], 64, 1)
+        zero = jnp.zeros((CHUNK, 128), F32)
+        q_val = [
+            jnp.where(low_half, zero, q_roll),
+            jnp.where(low_half, q_roll, pltpu.roll(tiles[1], 64, 1)),
+        ]
+        k_val = [jnp.where(low_half, zero, tiles[1]), tiles[2]]
+        v_val = [
+            jnp.where(low_half, zero, v_roll),
+            jnp.where(low_half, v_roll, pltpu.roll(tiles[4], 64, 1)),
+        ]
+        q_all[l, j] = jnp.concatenate(q_val, axis=1).astype(BF16)
+        k_all[l, j] = jnp.concatenate(k_val, axis=1).astype(BF16)
+        v_mat = jnp.concatenate(v_val, axis=1)
+        v_all[l, j] = v_mat.astype(BF16)
+        v_tr[:, pl.ds(pl.multiple_of(j * CHUNK, CHUNK), CHUNK)] = jnp.transpose(v_mat).astype(BF16)
+
+    def head_tile(mat, h):
+        if h == 0:
+            return mat[:, 0:128]
+        keep = low_half if h == 1 else jnp.logical_not(low_half)
+        return jnp.where(keep, mat[:, 128:256], jnp.zeros((), mat.dtype))
+
+    def tile_of(ref, l, h):
+        full = ref[l].reshape(ROWS, 256)
+        return full[:, 0:128] if h == 0 else full[:, 128:256]
+
+    def allowed_of(j):
+        col = kid_col[...].reshape(ROWS, 128)
+        return jnp.concatenate([col, col], axis=1) == kid_row[j, 0:1, :]
+
+    def attend_chunk(l, j):
+        allowed = allowed_of(j)
+        q_mat = q_all[l, j]
+        outs = [jnp.zeros((64, CHUNK), F32)]
+        for h in range(HEADS_DEV):
+            scores = dot_nt(tile_of(k_all, l, h), head_tile(q_mat, h)) * scale
+            scores = jnp.where(allowed, scores, big_negative)
+            top = jnp.max(scores, axis=0, keepdims=True)
+            expo = jnp.exp(scores - top)
+            tot = jnp.sum(expo, axis=0, keepdims=True)
+            lse_all[l, j, h : h + 1, :] = top + jnp.log(tot)
+            out = dot_nn(v_tr[64 + 64 * h : 128 + 64 * h, :], expo.astype(BF16))
+            outs.append(out / tot)
+        o_mat = jnp.transpose(jnp.concatenate(outs, axis=0)).astype(BF16)
+        o_all[l, j] = o_mat
+        send_partial(j, dot_nt(o_mat, wt[l, 0].reshape(D, D)[:, 512:768]))
+
+    def middle(l, j):
+        mid = res[2 * l, j] + total(j, 0) + vec(l, 4)
+        res[2 * l + 1, j] = mid
+        hat, _ = norm_rows(mid)
+        c_all[l, j, my_c] = (hat * vec(l, 2) + vec(l, 3)).astype(BF16)
+        own_copy(c_all.at[l], j).start()
+
+    def mlp(l, j):
+        own_copy(c_all.at[l], j).wait()
+        rows = c_all[l, j].reshape(CHUNK, D)
+        pre = dot_nn(rows, wt[l, 1].reshape(D, D)) + vec(l, 6)
+        cdf = 0.5 * (1.0 + lax.erf(pre * (1.0 / math.sqrt(2.0))))
+        pdf = jnp.exp(-0.5 * pre * pre) * (1.0 / math.sqrt(2.0 * math.pi))
+        act = (pre * cdf).astype(BF16)
+        z_all[l, j] = act
+        gp_all[l, j] = (cdf + pre * pdf).astype(BF16)
+
+        @pl.when(jnp.logical_and(l == 0, j == 0))
+        def _():
+            gather_finish(0, 2)
+
+        send_partial(j, dot_nt(z_all[l, j], wt[l, 2].reshape(D, D)))
+
+    def out_copies(ref, hbm, which, j):
+        return (
+            pltpu.make_async_copy(ref.at[j], hbm.at[j, my_c], out_sem.at[which, j]),
+            remote(ref.at[j], hbm.at[j, my_c], far_s.at[which, j], far_r.at[which, j], sibling),
+        )
+
+    def layer_end(l, j):
+        new = res[2 * l + 1, j] + total(j, 1) + vec(l, 5)
+
+        @pl.when(l < LAYERS - 1)
+        def _():
+            res[2 * LAYERS - 2, j] = new
+            hat, _ = norm_rows(new)
+            a_all[LAYERS - 1, j, my_c] = (hat * vec(LAYERS - 1, 0) + vec(LAYERS - 1, 1)).astype(BF16)
+            own_copy(a_all.at[LAYERS - 1], j).start()
+
+        @pl.when(l == LAYERS - 1)
+        def _():
+            x_out[j] = new
+            for copy in out_copies(x_out, bo_hbm, 0, j):
+                copy.start()
+
+    def when_chunk(tick, offset, func):
+        @pl.when(jnp.logical_and(tick >= offset, tick < offset + CHUNKS))
+        def _():
+            func(tick - offset)
+
+    def at(cond, func):
+        @pl.when(cond)
+        def _():
+            func()
+
+    def first_norm(j, carry):
+        load_rows(j, 0).wait()
+        load_rows(j, 1).wait()
+        hat, _ = norm_rows(res[0, j])
+        a_all[0, j, my_c] = (hat * vec(0, 0) + vec(0, 1)).astype(BF16)
+        hat, _ = norm_rows(res[1, j])
+        a_all[0, j, other_c] = (hat * vec(0, 0) + vec(0, 1)).astype(BF16)
+        return carry
+
+    lax.fori_loop(0, CHUNKS, first_norm, 0)
+    gather_forward(0, 0)
+    gather_finish(0, 0)
+
+    def first_project(j, carry):
+        project(0, j)
+        return carry
+
+    lax.fori_loop(0, CHUNKS, first_project, 0)
+
+    def forward_layer(l, carry):
+        def step(tick, inner):
+            when_chunk(tick, 1, lambda j: pass_on(j, 0))
+            when_chunk(tick, 5, lambda j: pass_on(j, 1))
+            when_chunk(tick, 3, lambda j: middle(l, j))
+            when_chunk(tick, 7, lambda j: layer_end(l, j))
+            when_chunk(tick, 0, lambda j: attend_chunk(l, j))
+
+            def next_project(j):
+                own_copy(a_all.at[LAYERS - 1], j).wait()
+                project(LAYERS - 1, j)
+
+            @pl.when(l == 0)
+            def _():
+                at(tick == 2, lambda: gather_forward(0, 1))
+
+                @pl.when(tick == 4)
+                def _():
+                    gather_finish(0, 1)
+                    gather_forward(0, 2)
+
+                at(tick == 6, lambda: gather_forward(1, 0))
+                at(tick == 8, lambda: gather_finish(1, 0))
+                at(tick == 9, lambda: gather_forward(1, 1))
+
+            @pl.when(l == 1)
+            def _():
+                at(tick == 3, lambda: gather_forward(1, 2))
+
+                @pl.when(tick == 4)
+                def _():
+                    gather_finish(1, 1)
+                    gather_finish(1, 2)
+
+            when_chunk(tick, 4, lambda j: mlp(l, j))
+
+            @pl.when(l == 0)
+            def _():
+                when_chunk(tick, 8, next_project)
+
+            return inner
+
+        lax.fori_loop(0, 12, step, 0)
+        return carry
+
+    lax.fori_loop(0, LAYERS, forward_layer, 0)
+
+    def load_cot(j):
+        return pltpu.make_async_copy(ct_hbm.at[j, my_c], y_own.at[j], ct_sem.at[j])
+
+    for j in range(CHUNKS):
+        load_cot(j).start()
+
+    def first_grad(j, carry):
+        load_cot(j).wait()
+        rows = jnp.where(kid_col[2 * j + my_c][:, 0:1] >= 0.0, y_own[j], 0.0)
+        y_own[j] = rows
+        y_all[j, my_c] = rows.astype(BF16)
+        own_copy(y_all, j).start()
+        return carry
+
+    lax.fori_loop(0, CHUNKS, first_grad, 0)
+
+    def add_vec(l, k, value):
+        gvecs[l, k : k + 1, :] += value
+
+    def mlp_back(l, j):
+        own_copy(y_all, j).wait()
+        d_act = dot_nn(y_all[j].reshape(CHUNK, D), wt[l, 2].reshape(D, D))
+        d_pre = (d_act * gp_all[l, j].astype(F32)).astype(BF16)
+        du_all[j] = d_pre
+        add_vec(l, 6, jnp.sum(d_pre.astype(F32), axis=0, keepdims=True))
+        send_partial(j, dot_nt(du_all[j], wt[l, 1].reshape(D, D)))
+
+    def middle_back(l, j):
+        grad = total(j, 0)
+        d_rows, d_gain, d_shift = norm_back(grad, res[2 * l + 1, j], vec(l, 2))
+        y_rows = y_own[j]
+        add_vec(l, 5, jnp.sum(y_rows, axis=0, keepdims=True))
+        g_rows = y_rows + d_rows
+        add_vec(l, 2, d_gain)
+        add_vec(l, 3, d_shift)
+        add_vec(l, 4, jnp.sum(g_rows, axis=0, keepdims=True))
+        y_own[j] = g_rows
+        g_all[j, my_c] = g_rows.astype(BF16)
+        own_copy(g_all, j).start()
+
+    def attend_back(l, j):
+        own_copy(g_all, j).wait()
+        d_out = dot_nn(g_all[j].reshape(CHUNK, D), wt[l, 0].reshape(D, D)[:, 512:768])
+        do_mat = d_out.astype(BF16)
+        prod = jnp.transpose(do_mat.astype(F32) * o_all[l, j].astype(F32))
+        allowed = allowed_of(j)
+        q_mat = q_all[l, j]
+        dq_parts = []
+        for h in range(HEADS_DEV):
+            q_h = head_tile(q_mat, h)
+            do_h = head_tile(do_mat, h)
+            scores = dot_nt(tile_of(k_all, l, h), q_h) * scale
+            scores = jnp.where(allowed, scores, big_negative)
+            probs = jnp.exp(scores - lse_all[l, j, h : h + 1, :])
+            delta = jnp.sum(prod[64 + 64 * h : 128 + 64 * h, :], axis=0, keepdims=True)
+            d_probs = dot_nt(tile_of(v_all, l, h), do_h)
+            d_scores = (probs * (d_probs - delta)).astype(BF16)
+            t = 0 if h == 0 else 128
+            dv_acc[:, t : t + 128] += dot_nn(probs.astype(BF16), do_h)
+            dk_acc[:, t : t + 128] += dot_nn(d_scores, q_h)
+            dq_parts.append(dot_nn(v_tr[64 + 64 * h : 128 + 64 * h, :], d_scores))
+        dq_parts.append(jnp.zeros((64, CHUNK), F32))
+        dq_mat = jnp.transpose(jnp.concatenate(dq_parts, axis=0) * scale)
+        dx_all[j, :, 0:256] = dq_mat.astype(BF16)
+
+    def project_back(l, j):
+        rows = pl.ds(pl.multiple_of(j * CHUNK, CHUNK), CHUNK)
+        dk_mat = dk_acc[rows, :] * scale
+        dv_mat = dv_acc[rows, :]
+        zero = jnp.zeros((CHUNK, 128), F32)
+        roll_zero = pltpu.roll(dv_mat[:, 0:128], 64, 1)
+        roll_one = pltpu.roll(dv_mat[:, 128:256], 64, 1)
+        tile_one = jnp.where(low_half, dx_all[j, :, 128:256].astype(F32), dk_mat[:, 0:128])
+        dx_all[j, :, 128:640] = jnp.concatenate(
+            [
+                tile_one,
+                dk_mat[:, 128:256],
+                jnp.where(low_half, roll_zero, roll_one),
+                jnp.where(low_half, roll_one, zero),
+            ],
+            axis=1,
+        ).astype(BF16)
+        dx_mat = dx_all[j]
+        gbias[l, 0:1, :] += jnp.sum(dx_mat.astype(F32), axis=0, keepdims=True)
+        send_partial(j, dot_nt(dx_mat, wt[l, 0].reshape(D, D)[:, 0:640]))
+
+    def layer_begin(l, j):
+        grad = total(j, 1)
+        d_rows, d_gain, d_shift = norm_back(grad, res[2 * l, j], vec(l, 0))
+        add_vec(l, 0, d_gain)
+        add_vec(l, 1, d_shift)
+        new = y_own[j] + d_rows
+        y_own[j] = new
+
+        @pl.when(l > 0)
+        def _():
+            y_all[j, my_c] = new.astype(BF16)
+            own_copy(y_all, j).start()
+
+        @pl.when(l == 0)
+        def _():
+            for copy in out_copies(y_own, ig_hbm, 1, j):
+                copy.start()
+
+    def slab(ref, p, owner):
+        return ref.at[p, pl.ds(pl.multiple_of(owner * B, B), B)]
+
+    def pair_copy(l, p, z):
+        dest = y_peers()[0]
+        return remote(
+            slab(dw, p, z * n_y + lax.rem(my_y + 1, n_y)),
+            rs_one.at[l, p, z],
+            p_s.at[l, p, z],
+            p_r.at[l, p, z],
+            dp_dev(dest),
+        )
+
+    def line_copy(l, p, s):
+        dest = z_peer(s)
+        return remote(
+            slab(dw, p, dest * n_y + my_y),
+            rs_two.at[l, p, n_z - 1 - s],
+            t_s.at[l, p, s - 1],
+            t_r.at[l, p, n_z - 1 - s],
+            dp_dev(dest * n_y + my_y),
+        )
+
+    def line_from(l, p, s):
+        return remote(
+            slab(dw, p, me),
+            rs_two.at[l, p, s - 1],
+            t_s.at[l, p, s - 1],
+            t_r.at[l, p, s - 1],
+            dp_dev(z_peer(s) * n_y + my_y),
+        )
+
+    def scatter_drain(l, p):
+        for z in range(n_z):
+            pair_copy(l, p, z).wait_send()
+        for s in range(1, n_z):
+            line_copy(l, p, s).wait_send()
+
+    def scatter_begin(l, p):
+        for z in range(n_z):
+            pair_copy(l, p, z).start()
+
+    def scatter_middle(l, p):
+        for s in list(range(1, n_z)) + [0]:
+            z = z_peer(s)
+            pair_copy(l, p, z).wait_recv()
+            ref = slab(dw, p, z * n_y + my_y)
+            ref[...] = (ref[...].astype(F32) + rs_one[l, p, z].astype(F32)).astype(BF16)
+            if s:
+                line_copy(l, p, s).start()
+
+    def block_copies(l, p):
+        runs = ((0, 6), (14, 2)) if p == 0 else ((PARTS[p][0], 8),)
+        return [
+            pltpu.make_async_copy(
+                g_out.at[l, pl.ds(first, count)],
+                gb_hbm.at[l, pl.ds(first, count)],
+                gout_sem.at[l, p + 3 * k],
+            )
+            for k, (first, count) in enumerate(runs)
+        ]
+
+    def scatter_end(l, p):
+        acc = slab(dw, p, me)[...].astype(F32)
+        for s in range(1, n_z):
+            line_from(l, p, s).wait_recv()
+            acc = acc + rs_two[l, p, s - 1].astype(F32)
+        nm_ref[0:1, 0:1] += jnp.sum(acc * acc, keepdims=True)
+        for b in range(8):
+            square = acc[:, B * b : B * b + B]
+            blk = PARTS[p][b]
+            g_out[l, blk, :, 0:B] = jnp.transpose(square) if blk in TRANSPOSED[p] else square
+        for copy in block_copies(l, p):
+            copy.start()
+
+    nm_ref[...] = jnp.zeros_like(nm_ref)
+
+    def weight_grad(l, p, func):
+        at(l < LAYERS - 1, lambda: scatter_drain(LAYERS - 1, p))
+
+        def piece(m, carry):
+            cols = pl.ds(pl.multiple_of(m * 256, 256), 256)
+            dw[p, cols, :] = func(cols).astype(BF16)
+            return carry
+
+        lax.fori_loop(0, D // 256, piece, 0)
+        scatter_begin(l, p)
+
+    def down_grad(l):
+        def func(cols):
+            return dot_tn(
+                y_all[:, :, :, cols].reshape(ROWS, 256), z_all[l].reshape(ROWS, D)
+            )
+
+        weight_grad(l, 2, func)
+
+    def up_grad(l):
+        def func(cols):
+            return dot_tn(
+                c_all[l, :, :, :, cols].reshape(ROWS, 256), du_all[...].reshape(ROWS, D)
+            )
+
+        weight_grad(l, 1, func)
+
+    def qkv_grad(l):
+        def func(cols):
+            first = dot_tn(
+                a_all[l, :, :, :, cols].reshape(ROWS, 256), dx_all[...].reshape(ROWS, 640)
+            )
+            second = dot_tn(
+                g_all[:, :, :, cols].reshape(ROWS, 256), o_all[l].reshape(ROWS, 256)
+            )
+            return jnp.concatenate(
+                [first[:, 0:512], first[:, 512:640] + second[:, 0:128], second[:, 128:256]], axis=1
+            )
+
+        weight_grad(l, 0, func)
+
+    def wait_blocks(l, p):
+        for copy in block_copies(l, p):
+            copy.wait()
+
+    def backward_layer(n, carry):
+        l = LAYERS - 1 - n
+        for j in range(CHUNKS):
+            v_tr[:, j * CHUNK : j * CHUNK + CHUNK] = jnp.transpose(k_all[l, j].astype(F32)).astype(
+                BF16
+            )
+        dk_acc[...] = jnp.zeros_like(dk_acc)
+        dv_acc[...] = jnp.zeros_like(dv_acc)
+
+        def step(tick, inner):
+            when_chunk(tick, 1, lambda j: pass_on(j, 0))
+            when_chunk(tick, 3, lambda j: middle_back(l, j))
+            when_chunk(tick, 0, lambda j: mlp_back(l, j))
+            at(tick == 3, lambda: down_grad(l))
+            at(tick == 4, lambda: up_grad(l))
+            when_chunk(tick, 4, lambda j: attend_back(l, j))
+            at(tick == 6, lambda: scatter_middle(l, 2))
+            at(tick == 7, lambda: scatter_middle(l, 1))
+            return inner
+
+        lax.fori_loop(0, 8, step, 0)
+
+        def step_two(tick, inner):
+            when_chunk(tick, 1, lambda j: pass_on(j, 1))
+            when_chunk(tick, 3, lambda j: layer_begin(l, j))
+            when_chunk(tick, 0, lambda j: project_back(l, j))
+            at(tick == 3, lambda: qkv_grad(l))
+
+            at(tick == 5, lambda: scatter_end(l, 2))
+
+            @pl.when(tick == 6)
+            def _():
+                scatter_end(l, 1)
+                scatter_middle(l, 0)
+
+            return inner
+
+        lax.fori_loop(0, 7, step_two, 0)
+        scatter_end(l, 0)
+        return carry
+
+    lax.fori_loop(0, LAYERS, backward_layer, 0)
+
+    sib = remote(gvecs, sib_in, sib_s.at[0], sib_r.at[0], sibling)
+    sib.start()
+    sib.wait()
+    row_at = lax.broadcasted_iota(jnp.int32, (8, D), 0)
+    for l in range(LAYERS):
+        mat = gvecs[l] + jnp.where(row_at < 6, sib_in[l], 0.0)
+        extra = gbias[l]
+        for s in range(n_dp):
+            gmsg_out[s, 8 * l : 8 * l + 8, 0:B] = mat[:, B * s : B * s + B]
+            gmsg_out[s, 8 * l : 8 * l + 8, 128:152] = extra[:, 24 * s : 24 * s + 24]
+            gmsg_out[s, 8 * l : 8 * l + 8, 152:176] = extra[:, 384 + 24 * s : 384 + 24 * s + 24]
+            gmsg_out[s, 8 * l : 8 * l + 8, B:128] = jnp.zeros((8, 128 - B), F32)
+            gmsg_out[s, 8 * l : 8 * l + 8, 176:256] = jnp.zeros((8, 80), F32)
+
+    def gmsg_copy(step):
+        dest = lax.rem(me + step, n_dp)
+        return remote(
+            gmsg_out.at[dest], gmsg_in.at[me], gm_s.at[step - 1], gm_r.at[me], dp_dev(dest)
+        )
+
+    def gmsg_from(step):
+        src = lax.rem(me + step, n_dp)
+        return remote(gmsg_out.at[src], gmsg_in.at[src], gm_s.at[step - 1], gm_r.at[src], dp_dev(src))
+
+    for step in range(1, n_dp):
+        gmsg_copy(step).start()
+    gmsg_in[me] = gmsg_out[me]
+    for step in range(1, n_dp):
+        gmsg_from(step).wait_recv()
+    summed = gmsg_in[0]
+    for s in range(1, n_dp):
+        summed = summed + gmsg_in[s]
+    sg_ref[...] = summed
+
+    squares = summed * summed
+    lane = lanes_of((1, 128))
+    packed = jnp.where(lane == 0, nm_ref[0:1, :], 0.0)
+    shared_sums = jnp.zeros((1, 128), F32)
+    for l in range(LAYERS):
+        base = 8 * l
+        up = jnp.sum(squares[base + 6 : base + 7, 0:B], keepdims=True)
+        query = jnp.sum(squares[base : base + 1, 128:152], keepdims=True)
+        value = jnp.sum(squares[base : base + 1, 152:176], keepdims=True)
+        for k, item in enumerate((query, value, up)):
+            packed = packed + jnp.where(lane == 1 + 3 * l + k, item, 0.0)
+        for r in range(6):
+            item = jnp.sum(squares[base + r : base + r + 1, 0:B], keepdims=True)
+            shared_sums = shared_sums + jnp.where(lane == 6 * l + r, item, 0.0)
+
+    for hop, dev in enumerate((sibling, across)):
+        nb_out[hop] = jnp.broadcast_to(packed, (8, 128))
+        swap = remote(nb_out.at[hop], nb_in.at[hop], nb_s.at[hop], nb_r.at[hop], dev)
+        swap.start()
+        swap.wait()
+        packed = packed + nb_in[hop, 0:1, :]
+    row8 = lax.broadcasted_iota(jnp.int32, (8, 128), 0)
+    nd_in[me] = jnp.where(row8 == 0, packed, jnp.where(row8 == 1, shared_sums, 0.0))
+
+    def nd_copy(step):
+        dest = lax.rem(me + step, n_dp)
+        return remote(nd_in.at[me], nd_in.at[me], nd_s.at[step - 1], nd_r.at[me], dp_dev(dest))
+
+    def nd_from(step):
+        src = lax.rem(me + step, n_dp)
+        return remote(nd_in.at[src], nd_in.at[src], nd_s.at[step - 1], nd_r.at[src], dp_dev(src))
+
+    for step in range(1, n_dp):
+        nd_copy(step).start()
+    for step in range(1, n_dp):
+        nd_from(step).wait_recv()
+    acc = nd_in[0]
+    for s in range(1, n_dp):
+        acc = acc + nd_in[s]
+    nm_ref[...] = acc
+
+    for p in range(3):
+        scatter_drain(0, p)
+        for l in range(LAYERS):
+            wait_blocks(l, p)
+            gather_drain(l, p)
+    for step in range(1, n_dp):
+        msg_copy(step).wait_send()
+        gmsg_copy(step).wait_send()
+        nd_copy(step).wait_send()
+    for j in range(CHUNKS):
+        for which, (ref, hbm) in enumerate(((x_out, bo_hbm), (y_own, ig_hbm))):
+            for copy in out_copies(ref, hbm, which, j):
+                copy.wait()
+
+
+def train_call(n_y, x_rows, ct_rows, seg, long_flag, blocks, split, shared):
+    hbm = pl.BlockSpec(memory_space=pl.ANY)
+    vmem = pl.BlockSpec(memory_space=pltpu.VMEM)
+    smem = pl.BlockSpec(memory_space=pltpu.SMEM)
+    dma = pltpu.SemaphoreType.DMA
+    n_dp = GROUPS
+    n_z = n_dp // n_y
+
+    def buf(shape, dtype=BF16):
+        return pltpu.VMEM(shape, dtype)
+
+    scratch = [
+        buf((LAYERS, 3, n_dp, B, D)),
+        buf((LAYERS, CHUNKS, 2, HALF, D)),
+        buf((LAYERS, CHUNKS, 2, HALF, D)),
+        buf((LAYERS, CHUNKS, CHUNK, 256)),
+        buf((LAYERS, CHUNKS, CHUNK, 256)),
+        buf((LAYERS, CHUNKS, CHUNK, 256)),
+        buf((256, ROWS)),
+        buf((LAYERS, CHUNKS, CHUNK, 256)),
+        buf((LAYERS, CHUNKS, 8, CHUNK), F32),
+        buf((LAYERS, CHUNKS, CHUNK, D)),
+        buf((LAYERS, CHUNKS, CHUNK, D)),
+        buf((2 * LAYERS, CHUNKS, HALF, D), F32),
+        buf((CHUNKS, HALF, D), F32),
+        buf((CHUNKS, 2, HALF, D)),
+        buf((CHUNKS, 2, HALF, D)),
+        buf((CHUNKS, CHUNK, D)),
+        buf((CHUNKS, CHUNK, 640)),
+        buf((ROWS, 256), F32),
+        buf((ROWS, 256), F32),
+        buf((CHUNKS, 2, HALF, D)),
+        buf((CHUNKS, HALF, D)),
+        buf((2, CHUNKS, HALF, D)),
+        buf((3, D, D)),
+        buf((LAYERS, 3, n_z, B, D)),
+        buf((LAYERS, 3, n_z - 1, B, D)),
+        buf((8, B, 128), F32),
+        buf((LAYERS, GROUP, B, 128), F32),
+        buf((CHUNKS, HALF, D), F32),
+        buf((8, HALF, 128), F32),
+        buf((CHUNKS, 8, CHUNK), F32),
+        buf((LAYERS, 8, D), F32),
+        buf((LAYERS, 8, 640), F32),
+        buf((LAYERS, 8, D), F32),
+        buf((LAYERS, 8, 640), F32),
+        buf((LAYERS, 8, D), F32),
+        buf((n_dp, 16, 256), F32),
+        buf((n_dp, 16, 256), F32),
+        buf((n_dp, 16, 256), F32),
+        buf((2, 8, 128), F32),
+        buf((2, 8, 128), F32),
+        buf((n_dp, 8, 128), F32),
+        dma((LAYERS, 3, 2 * n_z - 1)),
+        dma((LAYERS, 3, n_dp)),
+        dma((CHUNKS,)),
+        dma((CHUNKS,)),
+        dma((2, CHUNKS)),
+        dma((2, CHUNKS)),
+        dma((CHUNKS,)),
+        dma((CHUNKS,)),
+        dma((LAYERS, 3, n_z)),
+        dma((LAYERS, 3, n_z)),
+        dma((LAYERS, 3, n_z - 1)),
+        dma((LAYERS, 3, n_z - 1)),
+        dma((2, CHUNKS)),
+        dma((LAYERS,)),
+        dma((CHUNKS,)),
+        dma((2, CHUNKS)),
+        dma((2, CHUNKS)),
+        dma((2, CHUNKS)),
+        dma((LAYERS, 4)),
+        dma((n_dp - 1,)),
+        dma((n_dp,)),
+        dma((n_dp - 1,)),
+        dma((n_dp,)),
+        dma((1,)),
+        dma((1,)),
+        dma((2,)),
+        dma((2,)),
+        dma((n_dp - 1,)),
+        dma((n_dp,)),
+    ]
+    rows_shape = jax.ShapeDtypeStruct((CHUNKS, 2, HALF, D), F32)
+    return pl.pallas_call(
+        functools.partial(train_kernel, n_y),
+        out_shape=(
+            rows_shape,
+            rows_shape,
+            jax.ShapeDtypeStruct((LAYERS, GROUP, B, 128), F32),
+            jax.ShapeDtypeStruct((16, 256), F32),
+            jax.ShapeDtypeStruct((8, 128), F32),
+        ),
+        in_specs=[hbm, hbm, vmem, smem, hbm, vmem, vmem],
+        out_specs=(hbm, hbm, hbm, vmem, vmem),
+        scratch_shapes=scratch,
+        compiler_params=pltpu.CompilerParams(
+            collective_id=0, has_side_effects=True, vmem_limit_bytes=60 * 1024 * 1024
+        ),
+        cost_estimate=pl.CostEstimate(
+            flops=30_000_000_000, bytes_accessed=30_000_000, transcendentals=20_000_000
+        ),
+        name="train",
+    )(x_rows, ct_rows, seg, long_flag, blocks, split, shared)
+
+
+def update_kernel(
+    g_ref,
+    w_ref,
+    l_ref,
+    r_ref,
+    lr_ref,
+    rr_ref,
+    sg_ref,
+    nm_ref,
+    sp_ref,
+    sh_ref,
+    gout_ref,
+    nw_ref,
+    nl_ref,
+    nr_ref,
+    sgo_ref,
+    nsp_ref,
+    shg_ref,
+    nsh_ref,
+    norm_ref,
+    place,
+):
+    lane = lanes_of((1, 128))
+    row_zero = nm_ref[0:1, :]
+    row_one = nm_ref[1:2, :]
+    total_sq = jnp.sum(jnp.where(lane < 7, row_zero, 0.0), keepdims=True) + jnp.sum(
+        jnp.where(lane < 12, row_one, 0.0), keepdims=True
+    )
+    norm = jnp.sqrt(total_sq)
+    factor = clip_limit / jnp.maximum(norm, clip_limit)
+    squared = factor * factor
+
+    for b in range(g_ref.shape[1]):
+        grad = g_ref[0, b][:, 0:B]
+        low = grad.astype(BF16)
+        roots = []
+        for k, ref in enumerate((lr_ref, rr_ref)):
+            xs = [ref[0, b, pl.ds(m, 24, stride=3), :] for m in range(3)]
+            roots.append(flat_to_square(*xs, place.at[6 * b + k]))
+        left_gram = dot_nt(low, low)
+        right_gram = dot_tn(low, low)
+        partial_dir = dot_nn(roots[0].astype(BF16), low)
+        direction = dot_nn(partial_dir.astype(BF16), roots[1].astype(BF16)) * factor
+        mean_sq = jnp.mean(direction * direction, keepdims=True)
+        step = direction * (rate_matrix * lax.rsqrt(mean_sq + eps_norm))
+        grad_flat = square_to_flat(grad, place.at[6 * b + 2])
+        left_flat = square_to_flat(left_gram, place.at[6 * b + 3])
+        right_flat = square_to_flat(right_gram, place.at[6 * b + 4])
+        step_flat = square_to_flat(step, place.at[6 * b + 5])
+        weight = (1.0 - decay) * squared
+        for m in range(3):
+            rows = pl.ds(m, 24, stride=3)
+            gout_ref[0, b, rows, :] = grad_flat[m] * factor
+            nl_ref[0, b, rows, :] = decay * l_ref[0, b, rows, :] + weight * left_flat[m]
+            nr_ref[0, b, rows, :] = decay * r_ref[0, b, rows, :] + weight * right_flat[m]
+            nw_ref[0, b, rows, :] = w_ref[0, b, rows, :] - step_flat[m]
+
+    @pl.when((pl.program_id(0) == 0) & (pl.program_id(1) == 0))
+    def _():
+        norm_ref[...] = norm
+        sel = table_selector((144, 256))
+        col = lax.broadcasted_iota(jnp.int32, (8, 256), 1)
+        for l in range(LAYERS):
+            sums = [row_zero[:, 1 + 3 * l + k : 2 + 3 * l + k] for k in range(3)]
+            means = [sums[0] / D, sums[1] / D, sums[2] / FF]
+            scales = [lax.rsqrt(squared * m + eps_norm) for m in means]
+            src = sg_ref[8 * l : 8 * l + 8, :]
+            line = jnp.where(col[0:1] < 128, src[6:7, :], src[0:1, :]) * factor
+            step = line * jnp.where(
+                col[0:1] < 128, scales[2], jnp.where(col[0:1] < 152, scales[0], scales[1])
+            )
+            both = jnp.concatenate([line, step, jnp.zeros((6, 256), F32)], axis=0)
+            table = lax.dot_general(
+                both, sel, (((1,), (1,)), ((), ())), precision=highest, preferred_element_type=F32
+            )
+            sgo_ref[l : l + 1, :] = table[0:1, :]
+            nsp_ref[l : l + 1, :] = sp_ref[l : l + 1, :] - rate_vector * table[1:2, :]
+            for r in range(6):
+                mean = row_one[:, 6 * l + r : 6 * l + r + 1] / D
+                grad = src[r : r + 1, 0:B] * factor
+                shg_ref[6 * l + r : 6 * l + r + 1, :] = grad
+                nsh_ref[6 * l + r : 6 * l + r + 1, :] = sh_ref[
+                    6 * l + r : 6 * l + r + 1, :
+                ] - rate_vector * grad * lax.rsqrt(squared * mean + eps_norm)
+
+
+def update_call(grads, weights, left, right, left_roots, right_roots, sums, norms, split, shared):
+    per = 4
+    flat = pl.BlockSpec((1, per, 72, 128), lambda i, j: (i, j, 0, 0))
+    square = pl.BlockSpec((1, per, B, 128), lambda i, j: (i, j, 0, 0))
+
+    def whole(shape):
+        return pl.BlockSpec(shape, lambda i, j: (0,) * len(shape))
+
+    flat_shape = jax.ShapeDtypeStruct((LAYERS, GROUP, 72, 128), F32)
+    return pl.pallas_call(
+        update_kernel,
+        grid=(LAYERS, GROUP // per),
+        out_shape=(
+            flat_shape,
+            flat_shape,
+            flat_shape,
+            flat_shape,
+            jax.ShapeDtypeStruct((LAYERS, 144), F32),
+            jax.ShapeDtypeStruct((LAYERS, 144), F32),
+            jax.ShapeDtypeStruct((6 * LAYERS, B), F32),
+            jax.ShapeDtypeStruct((6 * LAYERS, B), F32),
+            jax.ShapeDtypeStruct((1, 1), F32),
+        ),
+        in_specs=[square, flat, flat, flat, flat, flat]
+        + [whole((16, 256)), whole((8, 128)), whole((LAYERS, 144)), whole((6 * LAYERS, B))],
+        out_specs=(
+            flat,
+            flat,
+            flat,
+            flat,
+            whole((LAYERS, 144)),
+            whole((LAYERS, 144)),
+            whole((6 * LAYERS, B)),
+            whole((6 * LAYERS, B)),
+            whole((1, 1)),
+        ),
+        scratch_shapes=[pltpu.VMEM((6 * per, B, 128), F32)],
+        compiler_params=pltpu.CompilerParams(vmem_limit_bytes=32 * 1024 * 1024),
+        name="update",
+    )(grads, weights, left, right, left_roots, right_roots, sums, norms, split, shared)
+
+
+def fast_body(
+    n_y,
+    tokens_in,
+    cotangent,
+    segment_ids,
+    long_seq,
+    weights,
+    left_stats,
+    right_stats,
+    left_roots,
+    right_roots,
+    split_params,
+    shared_params,
+):
+    rows = (CHUNKS, 2, HALF, D)
+    flat = (LAYERS, GROUP, 72, 128)
+    split = split_params.reshape(LAYERS, 144)
+    shared = shared_params.reshape(6 * LAYERS, B)
+    blocks = weights.reshape(flat)
+    out_rows, in_grad, grads, sums, norms = train_call(
+        n_y,
+        tokens_in.reshape(rows),
+        cotangent.reshape(rows),
+        segment_ids.reshape(8, 128),
+        long_seq.reshape(1, 1),
+        blocks,
+        split,
+        shared,
+    )
+    res = update_call(
+        grads,
+        blocks,
+        left_stats.reshape(flat),
+        right_stats.reshape(flat),
+        left_roots.reshape(flat),
+        right_roots.reshape(flat),
+        sums,
+        norms,
+        split,
+        shared,
+    )
+    mats = [r.reshape(weights.shape) for r in res[:4]]
+    return (
+        out_rows.reshape(tokens_in.shape),
+        in_grad.reshape(tokens_in.shape),
+        *mats,
+        res[4].reshape(split_params.shape),
+        res[5].reshape(split_params.shape),
+        res[6].reshape(shared_params.shape),
+        res[7].reshape(shared_params.shape),
+        res[8].reshape(()),
+    )
+
+
 def solution(mesh):
     in_specs = (
         P("dp", None),
@@ -449,4 +1620,7 @@
         P(None, None, "dp"),
         P(),
     )
-    return jax.shard_map(body, mesh=mesh, in_specs=in_specs, out_specs=out_specs, check_vma=False)
+    plan = body
+    if mesh.shape["dp"] == GROUPS and mesh.shape["tensor"] == 4:
+        plan = functools.partial(fast_body, 2)
+    return jax.shard_map(plan, mesh=mesh, in_specs=in_specs, out_specs=out_specs, check_vma=False)

time: 1690 us -> 352 us (0.21)
  waiting for transfers between devices: 855 us -> 0 us
  Pallas kernels: 0 us -> 332 us
  local copies, waits for them, and re-layouts: 345 us -> 18 us
  matrix products: 196 us -> 0 us
  other arithmetic: 136 us -> 0 us
  blocking collectives: 109 us -> 0 us
  between operations: 21.6 us -> 1.35 us
    unnamed x15 -> x0, waiting for transfers between devices: 493 us -> none
    pallas_call x0 -> x2, Pallas kernels: none -> 332 us  [the longest x1 318 us: train_call(): pl.pallas_call(functools.partial(train_kernel, n_y), out_shape=(rows_shap...]
    psum x8 -> x0, waiting for transfers between devices: 282 us -> none  [the longest x2 92 us: body(): normed_mid_grad = lax.psum(times_trans(pre_grad, up_weight), 'tensor')]
    dot_general x58 -> x0, matrix products: 196 us -> none  [the longest x8 35.5 us: matmul_low(): return jnp.dot(left_mat, right_mat, preferred_element_type=jnp.float32)]
    slice x16 -> x0, local copies, waits for them, and re-layouts: 115 us -> none  [the longest x1 45.8 us: body(): full_weights[layer_index, :, 0].astype(jnp.bfloat16)]
    all_gather x1 -> x0, waiting for transfers between devices: 80.9 us -> none  [body(): lax.all_gather(weights, 'dp', axis=1, tiled=True)]
    reshape x28 -> x3, local copies, waits for them, and re-layouts: 71.3 us -> 0.61 us  [the longest x1 0.6 us: fast_body(): shared = shared_params.reshape(6 * LAYERS, B)]
    all_gather x2 -> x0, blocking collectives: 69.4 us -> none  [the longest x1 34.9 us: body(): lax.all_gather(split_params, 'dp', axis=2, tiled=True)]
  transfers between devices with their start and end apart: 12 -> 0, of which waited for: 11 -> 0; matrix products, arithmetic and copies ran while one was open for 18% -> 0% of each run, Pallas kernels for 0% -> 0%
where the time goes in v1:
time: 352 us
  Pallas kernels  332 us (94%)
  local copies, waits for them, and re-layouts  18 us (5%)
    pallas_call x1, Pallas kernels, train_call(): pl.pallas_call(functools.partial(train_kernel, n_y), out_shape=(rows_shap...  318 us
    unnamed x30, local copies, waits for them, and re-layouts  17.4 us
    pallas_call x1, Pallas kernels, update_call(): pl.pallas_call(update_kernel, grid=(LAYERS, GROUP // per), out_shape=(fla...  14.1 us

profile of v1, /device:TPU:0, one launch (start us, length us, event | category | flops | bytes accessed | tf_op | source)
XLA Modules:
  0.0 351.6 jit_solution(11928287083279260950)
XLA Ops:
  1.3 1.3 copy.42
  2.6 0.7 copy.31
  3.2 0.6 reshape.94.shared_ref.sh_ref
  3.8 0.0 copy-start.1
  3.8 0.0 copy-start.2
  3.9 0.0 copy-start.6
  3.9 0.0 copy-start.8
  3.9 318.2 %train.1 = (f32[4,2,128,768]{3,2,1,0:T(8,128)}, f32[4,2,128,768]{3,2,1,0:T(8,128)}, f32[2,24,96,128]{3,2,1,0:T(8,128)}, f32[16,256]{1,0:T(8,128)}, f32[8,128]{1,0:T(8,128)}) custom-call(f32[4,2,128,768]{3,2,1,0:T(8,128)} %bitcast.34, f32[4,2,128,768]{3,2,1,0:T(8,128)} %bitcast.35, s32[8,128]{1,0:T(8,128)} %bitcast.40, s32[1,1]{1,0:T(1,128)} %bitcast.21.long_ref, ...), custom_call_target="tpu_custom_call" | custom-call | flops 30000001024 | bytes 30000000 | tf_op jit(solution)/shard_map/train/pallas_call | solution.py:1392
  322.0 0.0 copy-done.1
  322.0 0.0 copy-done.2
  322.0 0.0 copy-done.6
  322.0 0.0 copy-done.8
  322.1 0.0 copy-start
  322.1 1.7 copy-done
  323.7 0.0 copy-start.3
  323.7 1.5 copy-done.3
  325.2 0.0 copy-start.4
  325.2 1.5 copy-done.4
  326.7 0.0 copy-start.5
  326.7 1.5 copy-done.5
  328.2 0.0 copy-start.7
  328.2 0.7 copy-done.7
  328.9 0.0 copy-start.9
  328.9 0.7 copy-done.9
  329.6 14.1 %update.1 = (f32[2,24,72,128]{3,2,1,0:T(8,128)}, f32[2,24,72,128]{3,2,1,0:T(8,128)}, f32[2,24,72,128]{3,2,1,0:T(8,128)}, f32[2,24,72,128]{3,2,1,0:T(8,128)}, f32...) custom-call(f32[2,24,96,128]{3,2,1,0:T(8,128)S(1)} %copy-done, ...), custom_call_target="tpu_custom_call" | custom-call | tf_op jit(solution)/shard_map/update/pallas_call | solution.py:1509
  343.7 0.6 copy.36
  344.3 0.6 copy.37
  344.9 0.6 copy.38
  345.5 0.6 copy.39
  346.1 0.0 copy-start.10
  346.1 3.9 %copy.46 = f32[1024,768]{1,0:T(8,128)} copy(f32[1024,768]{1,0:T(8,128)} %bitcast.33) | data formatting | bytes 6291456
  350.0 0.0 copy-done.10
  350.0 1.7 copy.47
  (2 shorter events, 0.0 us)
Async XLA Ops:
  3.8 318.2 %copy-start.1 = (f32[2,24,1,9216]{3,2,1,0:T(1,128)S(1)}, f32[2,24,1,9216]{3,2,1,0:T(1,128)}, u32[]{:S(2)}) copy-start(f32[2,24,1,9216]{3,2,1,0:T(1,128)} %param.15) | copy-start | bytes 5308420
  3.8 318.2 %copy-start.2 = (f32[2,24,1,9216]{3,2,1,0:T(1,128)S(1)}, f32[2,24,1,9216]{3,2,1,0:T(1,128)}, u32[]{:S(2)}) copy-start(f32[2,24,1,9216]{3,2,1,0:T(1,128)} %param.16) | copy-start | bytes 5308420
  3.9 318.2 %copy-start.6 = (f32[12,96]{1,0:T(8,128)S(1)}, f32[12,96]{1,0:T(8,128)}, u32[]{:S(2)}) copy-start(f32[12,96]{1,0:T(8,128)} %reshape.94.shared_ref.sh_ref) | copy-start | bytes 13828
  3.9 318.2 %copy-start.8 = (f32[2,1,144]{2,0,1:T(2,128)S(1)}, f32[2,1,144]{2,0,1:T(2,128)}, u32[]{:S(2)}) copy-start(f32[2,1,144]{2,0,1:T(2,128)} %copy.42) | copy-start | bytes 3460
  322.1 1.7 copy-start
  323.7 1.5 copy-start.3
  325.2 1.5 copy-start.4
  326.7 1.5 copy-start.5
  328.2 0.7 copy-start.7
  328.9 0.7 copy-start.9
  346.1 3.9 %copy-start.10 = (f32[4,2,128,768]{3,2,1,0:T(8,128)S(1)}, f32[4,2,128,768]{3,2,1,0:T(8,128)}, u32[]{:S(2)}) copy-start(f32[4,2,128,768]{3,2,1,0:T(8,128)} %get-tuple-element.26) | copy-start | bytes 9437188

commit v2 on v1

--- a/solution.py
+++ b/solution.py
@@ -482,30 +482,38 @@
     return hit.astype(F32)
 
 
-def flat_to_square(x_zero, x_one, x_two, place):
+def flat_rows(ref):
+    x_zero, x_one, x_two = [ref[pl.ds(m, 24, stride=3), :] for m in range(3)]
     lane = lanes_of((24, 128))
-    place[pl.ds(0, 24, stride=4), :] = x_zero
-    place[pl.ds(1, 24, stride=4), :] = jnp.where(
-        lane < 32, pltpu.roll(x_zero, 32, 1), pltpu.roll(x_one, 32, 1)
-    )
-    place[pl.ds(2, 24, stride=4), :] = jnp.where(
-        lane < 64, pltpu.roll(x_one, 64, 1), pltpu.roll(x_two, 64, 1)
-    )
-    place[pl.ds(3, 24, stride=4), :] = pltpu.roll(x_two, 96, 1)
+    x_half = pltpu.roll(x_two, 64, 1)
+    return (
+        x_zero,
+        jnp.where(lane < 32, pltpu.roll(x_zero, 32, 1), pltpu.roll(x_one, 32, 1)),
+        jnp.where(lane < 64, pltpu.roll(x_one, 64, 1), x_half),
+        pltpu.roll(x_two, 96, 1),
+    )
+
+
+def flat_to_square(ref, place):
+    for m, rows in enumerate(flat_rows(ref)):
+        place[pl.ds(m, 24, stride=4), :] = rows
     return place[...][:, :B]
 
 
-def square_to_flat(square, place):
+def split_rows(square, place):
+    place[:, 0:B] = square
+    return jnp.concatenate([place[pl.ds(m, 24, stride=4), :] for m in range(4)], axis=0)[:, :B]
+
+
+def store_flat(ref, stacked):
     lane = lanes_of((24, 128))
-    place[:, 0:B] = square
-    m_zero, m_one, m_two, m_three = [place[pl.ds(m, 24, stride=4), :] for m in range(4)]
+    wide = jnp.concatenate([stacked, jnp.zeros((B, 128 - B), F32)], axis=1)
+    m_zero, m_one, m_two, m_three = [wide[24 * m : 24 * m + 24] for m in range(4)]
     one_back = pltpu.roll(m_one, 96, 1)
     two_back = pltpu.roll(m_two, 64, 1)
-    return (
-        jnp.where(lane < 96, m_zero, one_back),
-        jnp.where(lane < 64, one_back, two_back),
-        jnp.where(lane < 32, two_back, pltpu.roll(m_three, 32, 1)),
-    )
+    ref[pl.ds(0, 24, stride=3), :] = jnp.where(lane < 96, m_zero, one_back)
+    ref[pl.ds(1, 24, stride=3), :] = jnp.where(lane < 64, one_back, two_back)
+    ref[pl.ds(2, 24, stride=3), :] = jnp.where(lane < 32, two_back, pltpu.roll(m_three, 32, 1))
 
 
 def train_kernel(
@@ -515,11 +523,16 @@
     seg_ref,
     long_ref,
     w_hbm,
+    lr_hbm,
+    rr_hbm,
     split_ref,
     shared_ref,
     bo_hbm,
     ig_hbm,
-    gb_hbm,
+    gf_hbm,
+    lf_hbm,
+    rf_hbm,
+    pf_hbm,
     sg_ref,
     nm_ref,
     wt,
@@ -548,7 +561,8 @@
     rs_one,
     rs_two,
     place,
-    g_out,
+    flat,
+    g_acc,
     x_out,
     kid_col,
     kid_row,
@@ -578,10 +592,13 @@
     load_sem,
     land_sem,
     ct_sem,
+    y_s,
+    y_r,
     out_sem,
     far_s,
     far_r,
     gout_sem,
+    root_sem,
     m_s,
     m_r,
     gm_s,
@@ -615,20 +632,30 @@
             src_ref=src, dst_ref=dst, send_sem=send, recv_sem=recv, device_id=dev, device_id_type=MESH
         )
 
+    def at(cond, func):
+        @pl.when(cond)
+        def _():
+            func()
+
     def load_rows(j, which):
         half = my_c if which == 0 else other_c
         return pltpu.make_async_copy(x_hbm.at[j, half], res.at[which, j], load_sem.at[which, j])
 
     def load_blocks(l):
         return pltpu.make_async_copy(
-            w_hbm.at[l], g_out.at[l, :, pl.ds(0, 72)], land_sem.at[l]
-        )
+            w_hbm.at[l], flat.at[pl.ds(l * GROUP, GROUP)], land_sem.at[l]
+        )
+
+    def load_cot(j):
+        return pltpu.make_async_copy(ct_hbm.at[j, my_c], y_own.at[j], ct_sem.at[j])
 
     for l in range(LAYERS):
         load_blocks(l).start()
     for j in range(CHUNKS):
         load_rows(j, 0).start()
         load_rows(j, 1).start()
+    for j in range(CHUNKS):
+        load_cot(j).start()
 
     barrier = pltpu.get_barrier_semaphore()
     for step in range(1, n_dp):
@@ -641,14 +668,15 @@
     sel = table_selector((144, 256))
     for l in range(LAYERS):
         row = lax.dot_general(
-            jnp.broadcast_to(split_ref[l : l + 1, :], (8, 144)),
+            jnp.broadcast_to(split_ref[l], (8, 144)),
             sel,
             (((1,), (0,)), ((), ())),
             precision=highest,
             preferred_element_type=F32,
         )
         msg_in[me, 8 * l : 8 * l + 8, :] = row
-        msg_in[me, 8 * l : 8 * l + 6, 0:B] = shared_ref[6 * l : 6 * l + 6, :]
+        for r in range(6):
+            msg_in[me, 8 * l + r : 8 * l + r + 1, 0:B] = shared_ref[r, l : l + 1, :]
 
     pl.semaphore_wait(barrier, n_dp + 1)
 
@@ -673,16 +701,39 @@
     def y_peers():
         return [my_z * n_y + lax.rem(my_y + s, n_y) for s in range(1, n_y)]
 
-    def gather_begin(l, p):
-        for s in range(1, n_z):
-            gather_send(l, p, me, s - 1, z_peer(s) * n_y + my_y).start()
-        gather_send(l, p, me, n_z - 1, y_peers()[0]).start()
-
-    def gather_forward(l, p):
-        for s in range(1, n_z):
-            slab = z_peer(s) * n_y + my_y
-            gather_send(l, p, slab, n_z + s - 1, slab).wait_recv()
-            gather_send(l, p, slab, n_z + s - 1, y_peers()[0]).start()
+    def own_send(l, p):
+        @pl.when(my_z < n_z - 1)
+        def _():
+            gather_send(l, p, me, 0, me + n_y).start()
+
+        @pl.when(my_z > 0)
+        def _():
+            gather_send(l, p, me, 1, me - n_y).start()
+
+        gather_send(l, p, me, 2, y_peers()[0]).start()
+
+    def wave(l, p, hop):
+        @pl.when(my_z >= hop)
+        def _():
+            slab = me - hop * n_y
+            gather_send(l, p, slab, 0, slab).wait_recv()
+
+            @pl.when(my_z < n_z - 1)
+            def _():
+                gather_send(l, p, slab, 2 + hop, me + n_y).start()
+
+            gather_send(l, p, slab, n_z + 1 + hop, y_peers()[0]).start()
+
+        @pl.when(my_z + hop < n_z)
+        def _():
+            slab = me + hop * n_y
+            gather_send(l, p, slab, 0, slab).wait_recv()
+
+            @pl.when(my_z > 0)
+            def _():
+                gather_send(l, p, slab, 2 * n_z + hop, me - n_y).start()
+
+            gather_send(l, p, slab, 3 * n_z - 1 + hop, y_peers()[0]).start()
 
     def gather_finish(l, p):
         for s in range(0, n_z):
@@ -690,15 +741,25 @@
             gather_send(l, p, slab, 0, slab).wait_recv()
 
     def gather_drain(l, p):
-        for k in range(2 * n_z - 1):
+        def sent(k):
             gather_send(l, p, me, k, me).wait_send()
+
+        up, down = my_z < n_z - 1, my_z > 0
+        at(up, lambda: sent(0))
+        at(down, lambda: sent(1))
+        sent(2)
+        for hop in range(1, n_z):
+            low, high = my_z >= hop, my_z + hop < n_z
+            at(jnp.logical_and(low, up), lambda: sent(2 + hop))
+            at(low, lambda: sent(n_z + 1 + hop))
+            at(jnp.logical_and(high, down), lambda: sent(2 * n_z + hop))
+            at(high, lambda: sent(3 * n_z - 1 + hop))
 
     def relayout(l, p):
         cols = []
         for b in range(8):
             blk = PARTS[p][b]
-            xs = [g_out[l, blk, pl.ds(m, 24, stride=3), :] for m in range(3)]
-            square = flat_to_square(*xs, place.at[b])
+            square = flat_to_square(flat.at[l * GROUP + blk], place.at[b])
             cols.append(jnp.transpose(square) if blk in TRANSPOSED[p] else square)
         wt[l, p, me] = jnp.concatenate(cols, axis=1).astype(BF16)
 
@@ -706,7 +767,8 @@
         load_blocks(l).wait()
         for p in range(3):
             relayout(l, p)
-            gather_begin(l, p)
+            if p == 0:
+                at(l == 0, lambda: own_send(0, 0))
         return carry
 
     lax.fori_loop(0, LAYERS, relayout_layer, 0)
@@ -848,11 +910,13 @@
 
         send_partial(j, dot_nt(z_all[l, j], wt[l, 2].reshape(D, D)))
 
-    def out_copies(ref, hbm, which, j):
-        return (
-            pltpu.make_async_copy(ref.at[j], hbm.at[j, my_c], out_sem.at[which, j]),
-            remote(ref.at[j], hbm.at[j, my_c], far_s.at[which, j], far_r.at[which, j], sibling),
-        )
+    def near_copy(ref, hbm, which, j):
+        slot = j if which else lax.rem(j, 2)
+        return pltpu.make_async_copy(ref.at[slot], hbm.at[j, my_c], out_sem.at[which, j])
+
+    def far_copy(ref, hbm, which, j):
+        slot = j if which else lax.rem(j, 2)
+        return remote(ref.at[slot], hbm.at[j, my_c], far_s.at[which, j], far_r.at[which, j], sibling)
 
     def layer_end(l, j):
         new = res[2 * l + 1, j] + total(j, 1) + vec(l, 5)
@@ -866,107 +930,24 @@
 
         @pl.when(l == LAYERS - 1)
         def _():
-            x_out[j] = new
-            for copy in out_copies(x_out, bo_hbm, 0, j):
-                copy.start()
+            @pl.when(j >= 2)
+            def _():
+                near_copy(x_out, bo_hbm, 0, j - 2).wait()
+                far_copy(x_out, bo_hbm, 0, j - 2).wait_send()
+
+            x_out[lax.rem(j, 2)] = new
+            near_copy(x_out, bo_hbm, 0, j).start()
+            far_copy(x_out, bo_hbm, 0, j).start()
 
     def when_chunk(tick, offset, func):
         @pl.when(jnp.logical_and(tick >= offset, tick < offset + CHUNKS))
         def _():
             func(tick - offset)
 
-    def at(cond, func):
-        @pl.when(cond)
-        def _():
-            func()
-
-    def first_norm(j, carry):
-        load_rows(j, 0).wait()
-        load_rows(j, 1).wait()
-        hat, _ = norm_rows(res[0, j])
-        a_all[0, j, my_c] = (hat * vec(0, 0) + vec(0, 1)).astype(BF16)
-        hat, _ = norm_rows(res[1, j])
-        a_all[0, j, other_c] = (hat * vec(0, 0) + vec(0, 1)).astype(BF16)
-        return carry
-
-    lax.fori_loop(0, CHUNKS, first_norm, 0)
-    gather_forward(0, 0)
-    gather_finish(0, 0)
-
-    def first_project(j, carry):
-        project(0, j)
-        return carry
-
-    lax.fori_loop(0, CHUNKS, first_project, 0)
-
-    def forward_layer(l, carry):
-        def step(tick, inner):
-            when_chunk(tick, 1, lambda j: pass_on(j, 0))
-            when_chunk(tick, 5, lambda j: pass_on(j, 1))
-            when_chunk(tick, 3, lambda j: middle(l, j))
-            when_chunk(tick, 7, lambda j: layer_end(l, j))
-            when_chunk(tick, 0, lambda j: attend_chunk(l, j))
-
-            def next_project(j):
-                own_copy(a_all.at[LAYERS - 1], j).wait()
-                project(LAYERS - 1, j)
-
-            @pl.when(l == 0)
-            def _():
-                at(tick == 2, lambda: gather_forward(0, 1))
-
-                @pl.when(tick == 4)
-                def _():
-                    gather_finish(0, 1)
-                    gather_forward(0, 2)
-
-                at(tick == 6, lambda: gather_forward(1, 0))
-                at(tick == 8, lambda: gather_finish(1, 0))
-                at(tick == 9, lambda: gather_forward(1, 1))
-
-            @pl.when(l == 1)
-            def _():
-                at(tick == 3, lambda: gather_forward(1, 2))
-
-                @pl.when(tick == 4)
-                def _():
-                    gather_finish(1, 1)
-                    gather_finish(1, 2)
-
-            when_chunk(tick, 4, lambda j: mlp(l, j))
-
-            @pl.when(l == 0)
-            def _():
-                when_chunk(tick, 8, next_project)
-
-            return inner
-
-        lax.fori_loop(0, 12, step, 0)
-        return carry
-
-    lax.fori_loop(0, LAYERS, forward_layer, 0)
-
-    def load_cot(j):
-        return pltpu.make_async_copy(ct_hbm.at[j, my_c], y_own.at[j], ct_sem.at[j])
-
-    for j in range(CHUNKS):
-        load_cot(j).start()
-
-    def first_grad(j, carry):
-        load_cot(j).wait()
-        rows = jnp.where(kid_col[2 * j + my_c][:, 0:1] >= 0.0, y_own[j], 0.0)
-        y_own[j] = rows
-        y_all[j, my_c] = rows.astype(BF16)
-        own_copy(y_all, j).start()
-        return carry
-
-    lax.fori_loop(0, CHUNKS, first_grad, 0)
-
     def add_vec(l, k, value):
         gvecs[l, k : k + 1, :] += value
 
     def mlp_back(l, j):
-        own_copy(y_all, j).wait()
         d_act = dot_nn(y_all[j].reshape(CHUNK, D), wt[l, 2].reshape(D, D))
         d_pre = (d_act * gp_all[l, j].astype(F32)).astype(BF16)
         du_all[j] = d_pre
@@ -1047,8 +1028,8 @@
 
         @pl.when(l == 0)
         def _():
-            for copy in out_copies(y_own, ig_hbm, 1, j):
-                copy.start()
+            near_copy(y_own, ig_hbm, 1, j).start()
+            far_copy(y_own, ig_hbm, 1, j).start()
 
     def slab(ref, p, owner):
         return ref.at[p, pl.ds(pl.multiple_of(owner * B, B), B)]
@@ -1089,41 +1070,93 @@
             line_copy(l, p, s).wait_send()
 
     def scatter_begin(l, p):
-        for z in range(n_z):
-            pair_copy(l, p, z).start()
+        for s in list(range(1, n_z)) + [0]:
+            pair_copy(l, p, z_peer(s)).start()
 
     def scatter_middle(l, p):
         for s in list(range(1, n_z)) + [0]:
             z = z_peer(s)
             pair_copy(l, p, z).wait_recv()
             ref = slab(dw, p, z * n_y + my_y)
-            ref[...] = (ref[...].astype(F32) + rs_one[l, p, z].astype(F32)).astype(BF16)
+            both = (ref[...].astype(F32) + rs_one[l, p, z].astype(F32)).astype(BF16)
             if s:
+                ref[...] = both
                 line_copy(l, p, s).start()
+            else:
+                rs_one[l, p, my_z] = both
+
+    def runs_of(p):
+        return ((0, 0, 6), (6, 14, 2)) if p == 0 else ((0, PARTS[p][0], 8),)
 
     def block_copies(l, p):
-        runs = ((0, 6), (14, 2)) if p == 0 else ((PARTS[p][0], 8),)
         return [
             pltpu.make_async_copy(
-                g_out.at[l, pl.ds(first, count)],
-                gb_hbm.at[l, pl.ds(first, count)],
-                gout_sem.at[l, p + 3 * k],
+                flat.at[pl.ds(16 + 8 * k + here, count)],
+                hbm.at[l, pl.ds(there, count)],
+                gout_sem.at[k, n],
             )
-            for k, (first, count) in enumerate(runs)
+            for k, hbm in enumerate((gf_hbm, lf_hbm, rf_hbm, pf_hbm))
+            for n, (here, there, count) in enumerate(runs_of(p))
         ]
 
+    def root_copies(l, p):
+        return [
+            pltpu.make_async_copy(
+                hbm.at[l, pl.ds(there, count)],
+                flat.at[pl.ds(8 * k + here, count)],
+                root_sem.at[k, n],
+            )
+            for k, hbm in enumerate((lr_hbm, rr_hbm))
+            for n, (here, there, count) in enumerate(runs_of(p))
+        ]
+
     def scatter_end(l, p):
-        acc = slab(dw, p, me)[...].astype(F32)
+        acc = rs_one[l, p, my_z].astype(F32)
         for s in range(1, n_z):
             line_from(l, p, s).wait_recv()
             acc = acc + rs_two[l, p, s - 1].astype(F32)
         nm_ref[0:1, 0:1] += jnp.sum(acc * acc, keepdims=True)
+        g_acc[...] = acc
+
+    def block_update(l, p):
+        acc = g_acc[...]
+        for copy in root_copies(l, p):
+            copy.wait()
+        if p < 2:
+            for copy in block_copies(l, p + 1):
+                copy.wait()
+        else:
+            @pl.when(l < LAYERS - 1)
+            def _():
+                for copy in block_copies(LAYERS - 1, 0):
+                    copy.wait()
+
         for b in range(8):
             square = acc[:, B * b : B * b + B]
-            blk = PARTS[p][b]
-            g_out[l, blk, :, 0:B] = jnp.transpose(square) if blk in TRANSPOSED[p] else square
+            turned = jnp.transpose(square)
+            if PARTS[p][b] in TRANSPOSED[p]:
+                square, turned = turned, square
+            slot = 3 * (b % 2)
+            low = square.astype(BF16)
+            rows = split_rows(square, place.at[slot])
+            cols = split_rows(turned, place.at[slot + 1])
+            right = flat_to_square(flat.at[8 + b], place.at[slot + 2])
+            left = jnp.concatenate(flat_rows(flat.at[b]), axis=0)[:, :B]
+            store_flat(flat.at[16 + b], rows)
+            store_flat(flat.at[24 + b], dot_nt(rows.astype(BF16), low))
+            store_flat(flat.at[32 + b], dot_nn(cols.astype(BF16), low))
+            half = dot_nn(left.astype(BF16), low).astype(BF16)
+            store_flat(flat.at[40 + b], dot_nn(half, right.astype(BF16)))
         for copy in block_copies(l, p):
             copy.start()
+        if p > 0:
+            for copy in root_copies(l, p - 1):
+                copy.start()
+        else:
+            @pl.when(l > 0)
+            def _():
+                for copy in root_copies(0, 2):
+                    copy.start()
 
     nm_ref[...] = jnp.zeros_like(nm_ref)
 
@@ -1168,12 +1201,46 @@
 
         weight_grad(l, 0, func)
 
-    def wait_blocks(l, p):
-        for copy in block_copies(l, p):
-            copy.wait()
-
-    def backward_layer(n, carry):
-        l = LAYERS - 1 - n
+    def first_norm(j, carry):
+        load_rows(j, 0).wait()
+        load_rows(j, 1).wait()
+        hat, _ = norm_rows(res[0, j])
+        a_all[0, j, my_c] = (hat * vec(0, 0) + vec(0, 1)).astype(BF16)
+        hat, _ = norm_rows(res[1, j])
+        a_all[0, j, other_c] = (hat * vec(0, 0) + vec(0, 1)).astype(BF16)
+        return carry
+
+    def y_copy(j):
+        return remote(y_all.at[j, my_c], y_all.at[j, my_c], y_s.at[j], y_r.at[j], sibling)
+
+    def first_grad(j, carry):
+        load_cot(j).wait()
+        rows = jnp.where(kid_col[2 * j + my_c][:, 0:1] >= 0.0, y_own[j], 0.0)
+        y_own[j] = rows
+        y_all[j, my_c] = rows.astype(BF16)
+        y_copy(j).start()
+        return carry
+
+    def first_project(j, carry):
+        project(0, j)
+        return carry
+
+    for copy in root_copies(LAYERS - 1, 2):
+        copy.start()
+    wave(0, 0, 1)
+    own_send(0, 1)
+    lax.fori_loop(0, CHUNKS // 2, first_norm, 0)
+    wave(0, 0, 2)
+    lax.fori_loop(CHUNKS // 2, CHUNKS, first_norm, 0)
+    wave(0, 0, 3)
+    wave(0, 1, 1)
+    lax.fori_loop(0, CHUNKS, first_grad, 0)
+    gather_finish(0, 0)
+    wave(0, 1, 2)
+    own_send(0, 2)
+    lax.fori_loop(0, CHUNKS, first_project, 0)
+
+    def prepare_back(l):
         for j in range(CHUNKS):
             v_tr[:, j * CHUNK : j * CHUNK + CHUNK] = jnp.transpose(k_all[l, j].astype(F32)).astype(
                 BF16
@@ -1181,36 +1248,150 @@
         dk_acc[...] = jnp.zeros_like(dk_acc)
         dv_acc[...] = jnp.zeros_like(dv_acc)
 
+    def forward_layer(l, carry):
         def step(tick, inner):
             when_chunk(tick, 1, lambda j: pass_on(j, 0))
-            when_chunk(tick, 3, lambda j: middle_back(l, j))
-            when_chunk(tick, 0, lambda j: mlp_back(l, j))
-            at(tick == 3, lambda: down_grad(l))
-            at(tick == 4, lambda: up_grad(l))
-            when_chunk(tick, 4, lambda j: attend_back(l, j))
-            at(tick == 6, lambda: scatter_middle(l, 2))
-            at(tick == 7, lambda: scatter_middle(l, 1))
+            when_chunk(tick, 5, lambda j: pass_on(j, 1))
+
+            @pl.when(l == LAYERS - 1)
+            def _():
+                when_chunk(tick, 9, lambda j: pass_on(j, 0))
+
+            when_chunk(tick, 3, lambda j: middle(l, j))
+            when_chunk(tick, 7, lambda j: layer_end(l, j))
+            when_chunk(tick, 0, lambda j: attend_chunk(l, j))
+
+            def next_project(j):
+                own_copy(a_all.at[LAYERS - 1], j).wait()
+                project(LAYERS - 1, j)
+
+            def first_back(j):
+                far_copy(x_out, bo_hbm, 0, j).wait_recv()
+                y_copy(j).wait()
+                mlp_back(LAYERS - 1, j)
+
+            @pl.when(l == 0)
+            def _():
+                @pl.when(tick == 1)
+                def _():
+                    wave(0, 1, 3)
+                    wave(0, 2, 1)
+
+                @pl.when(tick == 3)
+                def _():
+                    wave(0, 2, 2)
+                    own_send(1, 0)
+
+                @pl.when(tick == 4)
+                def _():
+                    gather_finish(0, 1)
+                    wave(0, 2, 3)
+                    wave(1, 0, 1)
+
+                @pl.when(tick == 5)
+                def _():
+                    wave(1, 0, 2)
+                    own_send(1, 1)
+
+                @pl.when(tick == 7)
+                def _():
+                    wave(1, 0, 3)
+                    wave(1, 1, 1)
+
+                at(tick == 8, lambda: gather_finish(1, 0))
+
+                @pl.when(tick == 9)
+                def _():
+                    wave(1, 1, 2)
+                    own_send(1, 2)
+
+                @pl.when(tick == 11)
+                def _():
+                    wave(1, 1, 3)
+                    wave(1, 2, 1)
+
+            @pl.when(l == 1)
+            def _():
+                at(tick == 0, lambda: wave(1, 2, 2))
+                at(tick == 1, lambda: wave(1, 2, 3))
+
+                @pl.when(tick == 4)
+                def _():
+                    gather_finish(1, 1)
+                    gather_finish(1, 2)
+
+            when_chunk(tick, 4, lambda j: mlp(l, j))
+
+            @pl.when(l == 0)
+            def _():
+                when_chunk(tick, 8, next_project)
+
+            @pl.when(l == LAYERS - 1)
+            def _():
+                at(tick == 7, lambda: prepare_back(LAYERS - 1))
+                when_chunk(tick, 8, first_back)
+
             return inner
 
-        lax.fori_loop(0, 8, step, 0)
+        lax.fori_loop(0, 13, step, 0)
+        return carry
+
+    lax.fori_loop(0, LAYERS, forward_layer, 0)
+
+    def finish_part(l, p):
+        scatter_end(l, p)
+        block_update(l, p)
+
+    def backward_layer(n, carry):
+        l = LAYERS - 1 - n
+        upper = l == LAYERS - 1
+        lower = l < LAYERS - 1
+        down_grad(l)
+
+        @pl.when(lower)
+        def _():
+            scatter_middle(LAYERS - 1, 0)
+
+        def step(tick, inner):
+            middle_back(l, tick)
+            at(tick == 0, lambda: up_grad(l))
+
+            at(tick == 3, lambda: scatter_middle(l, 2))
+            attend_back(l, tick)
+            return inner
+
+        lax.fori_loop(0, CHUNKS, step, 0)
 
         def step_two(tick, inner):
             when_chunk(tick, 1, lambda j: pass_on(j, 1))
-            when_chunk(tick, 3, lambda j: layer_begin(l, j))
+
+            @pl.when(upper)
+            def _():
+                when_chunk(tick, 6, lambda j: pass_on(j, 0))
+
+            when_chunk(tick, 4, lambda j: layer_begin(l, j))
             when_chunk(tick, 0, lambda j: project_back(l, j))
             at(tick == 3, lambda: qkv_grad(l))
 
-            at(tick == 5, lambda: scatter_end(l, 2))
-
-            @pl.when(tick == 6)
+            @pl.when(lower)
             def _():
-                scatter_end(l, 1)
-                scatter_middle(l, 0)
-
+                at(tick == 4, lambda: finish_part(LAYERS - 1, 1))
+                at(tick == 5, lambda: finish_part(LAYERS - 1, 0))
+
+            def next_back(j):
+                own_copy(y_all, j).wait()
+                mlp_back(l - 1, j)
+
+            @pl.when(upper)
+            def _():
+                at(tick == 4, lambda: prepare_back(l - 1))
+                when_chunk(tick, 5, next_back)
+
+            at(tick == 5, lambda: scatter_middle(l, 1))
+            at(tick == 6, lambda: finish_part(l, 2))
             return inner
 
-        lax.fori_loop(0, 7, step_two, 0)
-        scatter_end(l, 0)
+        lax.fori_loop(0, 10, step_two, 0)
         return carry
 
     lax.fori_loop(0, LAYERS, backward_layer, 0)
@@ -1242,6 +1423,8 @@
     for step in range(1, n_dp):
         gmsg_copy(step).start()
     gmsg_in[me] = gmsg_out[me]
+    scatter_middle(0, 0)
+    finish_part(0, 1)
     for step in range(1, n_dp):
         gmsg_from(step).wait_recv()
     summed = gmsg_in[0]
@@ -1249,6 +1432,7 @@
         summed = summed + gmsg_in[s]
     sg_ref[...] = summed
 
+    scatter_end(0, 0)
     squares = summed * summed
     lane = lanes_of((1, 128))
     packed = jnp.where(lane == 0, nm_ref[0:1, :], 0.0)
@@ -1268,7 +1452,11 @@
         nb_out[hop] = jnp.broadcast_to(packed, (8, 128))
         swap = remote(nb_out.at[hop], nb_in.at[hop], nb_s.at[hop], nb_r.at[hop], dev)
         swap.start()
-        swap.wait()
+        if hop == 0:
+            swap.wait()
+        else:
+            block_update(0, 0)
+            swap.wait()
         packed = packed + nb_in[hop, 0:1, :]
     row8 = lax.broadcasted_iota(jnp.int32, (8, 128), 0)
     nd_in[me] = jnp.where(row8 == 0, packed, jnp.where(row8 == 1, shared_sums, 0.0))
@@ -1293,19 +1481,22 @@
     for p in range(3):
         scatter_drain(0, p)
         for l in range(LAYERS):
-            wait_blocks(l, p)
             gather_drain(l, p)
+    for copy in block_copies(0, 0):
+        copy.wait()
     for step in range(1, n_dp):
         msg_copy(step).wait_send()
         gmsg_copy(step).wait_send()
         nd_copy(step).wait_send()
     for j in range(CHUNKS):
-        for which, (ref, hbm) in enumerate(((x_out, bo_hbm), (y_own, ig_hbm))):
-            for copy in out_copies(ref, hbm, which, j):
-                copy.wait()
-
-
-def train_call(n_y, x_rows, ct_rows, seg, long_flag, blocks, split, shared):
+        if j >= 2:
+            near_copy(x_out, bo_hbm, 0, j).wait()
+            far_copy(x_out, bo_hbm, 0, j).wait_send()
+        near_copy(y_own, ig_hbm, 1, j).wait()
+        far_copy(y_own, ig_hbm, 1, j).wait()
+
+
+def train_call(n_y, x_rows, ct_rows, seg, long_flag, blocks, left, right, split, shared):
     hbm = pl.BlockSpec(memory_space=pl.ANY)
     vmem = pl.BlockSpec(memory_space=pltpu.VMEM)
     smem = pl.BlockSpec(memory_space=pltpu.SMEM)
@@ -1343,8 +1534,9 @@
         buf((LAYERS, 3, n_z, B, D)),
         buf((LAYERS, 3, n_z - 1, B, D)),
         buf((8, B, 128), F32),
-        buf((LAYERS, GROUP, B, 128), F32),
-        buf((CHUNKS, HALF, D), F32),
+        buf((LAYERS * GROUP, 72, 128), F32),
+        buf((B, D), F32),
+        buf((2, HALF, D), F32),
         buf((8, HALF, 128), F32),
         buf((CHUNKS, 8, CHUNK), F32),
         buf((LAYERS, 8, D), F32),
@@ -1358,7 +1550,7 @@
         buf((2, 8, 128), F32),
         buf((2, 8, 128), F32),
         buf((n_dp, 8, 128), F32),
-        dma((LAYERS, 3, 2 * n_z - 1)),
+        dma((LAYERS, 3, 4 * n_z)),
         dma((LAYERS, 3, n_dp)),
         dma((CHUNKS,)),
         dma((CHUNKS,)),
@@ -1373,10 +1565,13 @@
         dma((2, CHUNKS)),
         dma((LAYERS,)),
         dma((CHUNKS,)),
+        dma((CHUNKS,)),
+        dma((CHUNKS,)),
         dma((2, CHUNKS)),
         dma((2, CHUNKS)),
         dma((2, CHUNKS)),
-        dma((LAYERS, 4)),
+        dma((4, 2)),
+        dma((2, 2)),
         dma((n_dp - 1,)),
         dma((n_dp,)),
         dma((n_dp - 1,)),
@@ -1394,12 +1589,12 @@
         out_shape=(
             rows_shape,
             rows_shape,
-            jax.ShapeDtypeStruct((LAYERS, GROUP, B, 128), F32),
+            *[jax.ShapeDtypeStruct((LAYERS, GROUP, 72, 128), F32)] * 4,
             jax.ShapeDtypeStruct((16, 256), F32),
             jax.ShapeDtypeStruct((8, 128), F32),
         ),
-        in_specs=[hbm, hbm, vmem, smem, hbm, vmem, vmem],
-        out_specs=(hbm, hbm, hbm, vmem, vmem),
+        in_specs=[hbm, hbm, vmem, smem, hbm, hbm, hbm, vmem, vmem],
+        out_specs=(hbm, hbm, hbm, hbm, hbm, hbm, vmem, vmem),
         scratch_shapes=scratch,
         compiler_params=pltpu.CompilerParams(
             collective_id=0, has_side_effects=True, vmem_limit_bytes=60 * 1024 * 1024
@@ -1408,20 +1603,23 @@
             flops=30_000_000_000, bytes_accessed=30_000_000, transcendentals=20_000_000
         ),
         name="train",
-    )(x_rows, ct_rows, seg, long_flag, blocks, split, shared)
+    )(x_rows, ct_rows, seg, long_flag, blocks, left, right, split, shared)
 
 
 def update_kernel(
     g_ref,
+    lg_ref,
+    rg_ref,
+    p_ref,
     w_ref,
     l_ref,
     r_ref,
-    lr_ref,
-    rr_ref,
     sg_ref,
     nm_ref,
     sp_ref,
     sh_ref,
+    bo_ref,
+    ig_ref,
     gout_ref,
     nw_ref,
     nl_ref,
@@ -1431,8 +1629,12 @@
     shg_ref,
     nsh_ref,
     norm_ref,
-    place,
+    bo_out,
+    ig_out,
 ):
+    step_at = pl.program_id(0)
+    bo_out[...] = bo_ref[...]
+    ig_out[...] = ig_ref[...]
     lane = lanes_of((1, 128))
     row_zero = nm_ref[0:1, :]
     row_one = nm_ref[1:2, :]
@@ -1442,101 +1644,77 @@
     norm = jnp.sqrt(total_sq)
     factor = clip_limit / jnp.maximum(norm, clip_limit)
     squared = factor * factor
-
-    for b in range(g_ref.shape[1]):
-        grad = g_ref[0, b][:, 0:B]
-        low = grad.astype(BF16)
-        roots = []
-        for k, ref in enumerate((lr_ref, rr_ref)):
-            xs = [ref[0, b, pl.ds(m, 24, stride=3), :] for m in range(3)]
-            roots.append(flat_to_square(*xs, place.at[6 * b + k]))
-        left_gram = dot_nt(low, low)
-        right_gram = dot_tn(low, low)
-        partial_dir = dot_nn(roots[0].astype(BF16), low)
-        direction = dot_nn(partial_dir.astype(BF16), roots[1].astype(BF16)) * factor
-        mean_sq = jnp.mean(direction * direction, keepdims=True)
-        step = direction * (rate_matrix * lax.rsqrt(mean_sq + eps_norm))
-        grad_flat = square_to_flat(grad, place.at[6 * b + 2])
-        left_flat = square_to_flat(left_gram, place.at[6 * b + 3])
-        right_flat = square_to_flat(right_gram, place.at[6 * b + 4])
-        step_flat = square_to_flat(step, place.at[6 * b + 5])
-        weight = (1.0 - decay) * squared
-        for m in range(3):
-            rows = pl.ds(m, 24, stride=3)
-            gout_ref[0, b, rows, :] = grad_flat[m] * factor
-            nl_ref[0, b, rows, :] = decay * l_ref[0, b, rows, :] + weight * left_flat[m]
-            nr_ref[0, b, rows, :] = decay * r_ref[0, b, rows, :] + weight * right_flat[m]
-            nw_ref[0, b, rows, :] = w_ref[0, b, rows, :] - step_flat[m]
-
-    @pl.when((pl.program_id(0) == 0) & (pl.program_id(1) == 0))
+    gram_weight = (1.0 - decay) * squared
+
+    for b in range(g_ref.shape[0]):
+        gout_ref[b] = g_ref[b] * factor
+        nl_ref[b] = decay * l_ref[b] + gram_weight * lg_ref[b]
+        nr_ref[b] = decay * r_ref[b] + gram_weight * rg_ref[b]
+        direction = p_ref[b] * factor
+        mean_sq = jnp.sum(direction * direction, keepdims=True) / (B * B)
+        nw_ref[b] = w_ref[b] - direction * (rate_matrix * lax.rsqrt(mean_sq + eps_norm))
+
+    @pl.when(step_at == 0)
     def _():
         norm_ref[...] = norm
         sel = table_selector((144, 256))
-        col = lax.broadcasted_iota(jnp.int32, (8, 256), 1)
+        col = lanes_of((1, 256))
         for l in range(LAYERS):
             sums = [row_zero[:, 1 + 3 * l + k : 2 + 3 * l + k] for k in range(3)]
             means = [sums[0] / D, sums[1] / D, sums[2] / FF]
             scales = [lax.rsqrt(squared * m + eps_norm) for m in means]
             src = sg_ref[8 * l : 8 * l + 8, :]
-            line = jnp.where(col[0:1] < 128, src[6:7, :], src[0:1, :]) * factor
-            step = line * jnp.where(
-                col[0:1] < 128, scales[2], jnp.where(col[0:1] < 152, scales[0], scales[1])
-            )
+            line = jnp.where(col < 128, src[6:7, :], src[0:1, :]) * factor
+            step = line * jnp.where(col < 128, scales[2], jnp.where(col < 152, scales[0], scales[1]))
             both = jnp.concatenate([line, step, jnp.zeros((6, 256), F32)], axis=0)
             table = lax.dot_general(
                 both, sel, (((1,), (1,)), ((), ())), precision=highest, preferred_element_type=F32
             )
-            sgo_ref[l : l + 1, :] = table[0:1, :]
-            nsp_ref[l : l + 1, :] = sp_ref[l : l + 1, :] - rate_vector * table[1:2, :]
+            sgo_ref[l] = table[0:1, :]
+            nsp_ref[l] = sp_ref[l] - rate_vector * table[1:2, :]
             for r in range(6):
                 mean = row_one[:, 6 * l + r : 6 * l + r + 1] / D
                 grad = src[r : r + 1, 0:B] * factor
-                shg_ref[6 * l + r : 6 * l + r + 1, :] = grad
-                nsh_ref[6 * l + r : 6 * l + r + 1, :] = sh_ref[
-                    6 * l + r : 6 * l + r + 1, :
-                ] - rate_vector * grad * lax.rsqrt(squared * mean + eps_norm)
-
-
-def update_call(grads, weights, left, right, left_roots, right_roots, sums, norms, split, shared):
-    per = 4
-    flat = pl.BlockSpec((1, per, 72, 128), lambda i, j: (i, j, 0, 0))
-    square = pl.BlockSpec((1, per, B, 128), lambda i, j: (i, j, 0, 0))
+                shg_ref[r, l : l + 1, :] = grad
+                nsh_ref[r, l : l + 1, :] = sh_ref[r, l : l + 1, :] - rate_vector * grad * lax.rsqrt(
+                    squared * mean + eps_norm
+                )
+
+
+def update_call(grads, lefts, rights, dirs, weights, left, right, sums, norms, split, shared, outs):
+    per = 6
+    count = LAYERS * GROUP
+    flat = pl.BlockSpec((per, 72, 128), lambda i: (i, 0, 0))
+    rows = pl.BlockSpec((2 * HALF * CHUNKS * per // count, D), lambda i: (i, 0))
 
     def whole(shape):
-        return pl.BlockSpec(shape, lambda i, j: (0,) * len(shape))
-
-    flat_shape = jax.ShapeDtypeStruct((LAYERS, GROUP, 72, 128), F32)
+        return pl.BlockSpec(shape, lambda i: (0,) * len(shape))
+
+    flat_shape = jax.ShapeDtypeStruct((count, 72, 128), F32)
+    split_shape, shared_shape = (LAYERS, 1, 144), (6, LAYERS, B)
     return pl.pallas_call(
         update_kernel,
-        grid=(LAYERS, GROUP // per),
+        grid=(count // per,),
         out_shape=(
-            flat_shape,
-            flat_shape,
-            flat_shape,
-            flat_shape,
-            jax.ShapeDtypeStruct((LAYERS, 144), F32),
-            jax.ShapeDtypeStruct((LAYERS, 144), F32),
-            jax.ShapeDtypeStruct((6 * LAYERS, B), F32),
-            jax.ShapeDtypeStruct((6 * LAYERS, B), F32),
+            *[flat_shape] * 4,
+            *[jax.ShapeDtypeStruct(split_shape, F32)] * 2,
+            *[jax.ShapeDtypeStruct(shared_shape, F32)] * 2,
             jax.ShapeDtypeStruct((1, 1), F32),
+            *[jax.ShapeDtypeStruct(o.shape, F32) for o in outs],
         ),
-        in_specs=[square, flat, flat, flat, flat, flat]
-        + [whole((16, 256)), whole((8, 128)), whole((LAYERS, 144)), whole((6 * LAYERS, B))],
+        in_specs=[flat] * 7
+        + [whole((16, 256)), whole((8, 128)), whole(split_shape), whole(shared_shape), rows, rows],
         out_specs=(
-            flat,
-            flat,
-            flat,
-            flat,
-            whole((LAYERS, 144)),
-            whole((LAYERS, 144)),
-            whole((6 * LAYERS, B)),
-            whole((6 * LAYERS, B)),
+            *[flat] * 4,
+            *[whole(split_shape)] * 2,
+            *[whole(shared_shape)] * 2,
             whole((1, 1)),
+            rows,
+            rows,
         ),
-        scratch_shapes=[pltpu.VMEM((6 * per, B, 128), F32)],
-        compiler_params=pltpu.CompilerParams(vmem_limit_bytes=32 * 1024 * 1024),
+        compiler_params=pltpu.CompilerParams(vmem_limit_bytes=60 * 1024 * 1024),
         name="update",
-    )(grads, weights, left, right, left_roots, right_roots, sums, norms, split, shared)
+    )(grads, lefts, rights, dirs, weights, left, right, sums, norms, split, shared, *outs)
 
 
 def fast_body(
@@ -1555,40 +1733,38 @@
 ):
     rows = (CHUNKS, 2, HALF, D)
     flat = (LAYERS, GROUP, 72, 128)
-    split = split_params.reshape(LAYERS, 144)
-    shared = shared_params.reshape(6 * LAYERS, B)
-    blocks = weights.reshape(flat)
-    out_rows, in_grad, grads, sums, norms = train_call(
+    blocks = (LAYERS * GROUP, 72, 128)
+    split = split_params
+    shared = jnp.transpose(shared_params, (1, 0, 2))
+    out_rows, in_grad, grads, lefts, rights, dirs, sums, norms = train_call(
         n_y,
         tokens_in.reshape(rows),
         cotangent.reshape(rows),
         segment_ids.reshape(8, 128),
         long_seq.reshape(1, 1),
-        blocks,
+        weights.reshape(flat),
+        left_roots.reshape(flat),
+        right_roots.reshape(flat),
         split,
         shared,
     )
     res = update_call(
-        grads,
-        blocks,
-        left_stats.reshape(flat),
-        right_stats.reshape(flat),
-        left_roots.reshape(flat),
-        right_roots.reshape(flat),
+        *[m.reshape(blocks) for m in (grads, lefts, rights, dirs, weights, left_stats, right_stats)],
         sums,
         norms,
         split,
         shared,
+        (out_rows.reshape(tokens_in.shape), in_grad.reshape(tokens_in.shape)),
     )
     mats = [r.reshape(weights.shape) for r in res[:4]]
     return (
-        out_rows.reshape(tokens_in.shape),
-        in_grad.reshape(tokens_in.shape),
+        res[9],
+        res[10],
         *mats,
-        res[4].reshape(split_params.shape),
-        res[5].reshape(split_params.shape),
-        res[6].reshape(shared_params.shape),
-        res[7].reshape(shared_params.shape),
+        res[4],
+        res[5],
+        jnp.transpose(res[6], (1, 0, 2)),
+        jnp.transpose(res[7], (1, 0, 2)),
         res[8].reshape(()),
     )
 

time: 352 us -> 266 us (0.76)
  Pallas kernels: 332 us -> 264 us
  local copies, waits for them, and re-layouts: 18 us -> 0 us
    pallas_call x1, Pallas kernels: 318 us -> 250 us  [train_call(): pl.pallas_call(functools.partial(train_kernel, n_y), out_shape=(rows_shap...]
    unnamed x30 -> x0, local copies, waits for them, and re-layouts: 17.4 us -> none
where the time goes in v2:
time: 266 us
  Pallas kernels  264 us (99%)
    pallas_call x1, Pallas kernels, train_call(): pl.pallas_call(functools.partial(train_kernel, n_y), out_shape=(rows_shap...  250 us
    pallas_call x1, Pallas kernels, update_call(): pl.pallas_call(update_kernel, grid=(count // per,), out_shape=(*[flat_sha...  14.6 us

profile of v2, /device:TPU:0, one launch (start us, length us, event | category | flops | bytes accessed | tf_op | source)
XLA Modules:
  0.0 265.7 jit_solution(3648557564468193269)
XLA Ops:
  1.3 249.7 %train.1 = (f32[4,2,128,768]{3,2,1,0:T(8,128)}, f32[4,2,128,768]{3,2,1,0:T(8,128)}, f32[2,24,72,128]{3,2,1,0:T(8,128)}, f32[2,24,72,128]{3,2,1,0:T(8,128)}, f32[...) custom-call(f32[4,2,128,768]{3,2,1,0:T(8,128)} %bitcast.37, ...), custom_call_target="tpu_custom_call" | custom-call | flops 30000001024 | bytes 30000000 | tf_op jit(solution)/shard_map/train/pallas_call | solution.py:1587
  251.0 14.6 %update.1 = (f32[48,72,128]{2,1,0:T(8,128)}, f32[48,72,128]{2,1,0:T(8,128)}, f32[48,72,128]{2,1,0:T(8,128)}, f32[48,72,128]{2,1,0:T(8,128)}, f32[2,1,144]{2,1,0:...) custom-call(f32[48,72,128]{2,1,0:T(8,128)} %bitcast.31, ...), custom_call_target="tpu_custom_call" | custom-call | tf_op jit(solution)/shard_map/update/pallas_call | solution.py:1695

commit v3 on v2

--- a/solution.py
+++ b/solution.py
@@ -557,13 +557,13 @@
     stage,
     core_in,
     x_in,
+    side_in,
     dw,
     rs_one,
     rs_two,
     place,
     flat,
     g_acc,
-    x_out,
     kid_col,
     kid_row,
     vecs,
@@ -572,7 +572,6 @@
     gbias,
     sib_in,
     msg_in,
-    gmsg_in,
     gmsg_out,
     nb_out,
     nb_in,
@@ -759,7 +758,7 @@
         cols = []
         for b in range(8):
             blk = PARTS[p][b]
-            square = flat_to_square(flat.at[l * GROUP + blk], place.at[b])
+            square = flat_to_square(flat.at[l * GROUP + blk], place.at[b % 6])
             cols.append(jnp.transpose(square) if blk in TRANSPOSED[p] else square)
         wt[l, p, me] = jnp.concatenate(cols, axis=1).astype(BF16)
 
@@ -814,6 +813,8 @@
         return remote(stage.at[j, other_c], core_in.at[j], c_s.at[j], c_r.at[j], sibling)
 
     def x_copy(j, par):
+        if par == 2:
+            return remote(stage.at[j, my_c], side_in.at[j], x_s.at[2, j], x_r.at[2, j], across)
         return remote(stage.at[j, my_c], x_in.at[par, j], x_s.at[par, j], x_r.at[par, j], across)
 
     def own_copy(ref, j):
@@ -831,7 +832,8 @@
 
     def total(j, par):
         x_copy(j, par).wait()
-        return stage[j, my_c].astype(F32) + x_in[par, j].astype(F32)
+        came = side_in[j] if par == 2 else x_in[par, j]
+        return stage[j, my_c].astype(F32) + came.astype(F32)
 
     def project(l, j):
         rows = a_all[l, j].reshape(CHUNK, D)
@@ -904,40 +906,40 @@
         z_all[l, j] = act
         gp_all[l, j] = (cdf + pre * pdf).astype(BF16)
 
-        @pl.when(jnp.logical_and(l == 0, j == 0))
+        @pl.when(l < LAYERS - 1)
         def _():
-            gather_finish(0, 2)
-
-        send_partial(j, dot_nt(z_all[l, j], wt[l, 2].reshape(D, D)))
+            at(j == 0, lambda: gather_finish(0, 2))
+            send_partial(j, dot_nt(z_all[l, j], wt[l, 2].reshape(D, D)))
+
+        @pl.when(l == LAYERS - 1)
+        def _():
+            y_copy(j).wait()
+            mlp_back(LAYERS - 1, j)
+
+    def y_copy(j):
+        return remote(y_all.at[j, my_c], y_all.at[j, my_c], y_s.at[j], y_r.at[j], sibling)
 
     def near_copy(ref, hbm, which, j):
-        slot = j if which else lax.rem(j, 2)
-        return pltpu.make_async_copy(ref.at[slot], hbm.at[j, my_c], out_sem.at[which, j])
+        return pltpu.make_async_copy(ref.at[j], hbm.at[j, my_c], out_sem.at[which, j])
 
     def far_copy(ref, hbm, which, j):
-        slot = j if which else lax.rem(j, 2)
-        return remote(ref.at[slot], hbm.at[j, my_c], far_s.at[which, j], far_r.at[which, j], sibling)
+        return remote(ref.at[j], hbm.at[j, my_c], far_s.at[which, j], far_r.at[which, j], sibling)
 
     def layer_end(l, j):
         new = res[2 * l + 1, j] + total(j, 1) + vec(l, 5)
-
-        @pl.when(l < LAYERS - 1)
-        def _():
-            res[2 * LAYERS - 2, j] = new
-            hat, _ = norm_rows(new)
-            a_all[LAYERS - 1, j, my_c] = (hat * vec(LAYERS - 1, 0) + vec(LAYERS - 1, 1)).astype(BF16)
-            own_copy(a_all.at[LAYERS - 1], j).start()
-
-        @pl.when(l == LAYERS - 1)
-        def _():
-            @pl.when(j >= 2)
-            def _():
-                near_copy(x_out, bo_hbm, 0, j - 2).wait()
-                far_copy(x_out, bo_hbm, 0, j - 2).wait_send()
-
-            x_out[lax.rem(j, 2)] = new
-            near_copy(x_out, bo_hbm, 0, j).start()
-            far_copy(x_out, bo_hbm, 0, j).start()
+        res[2 * l + 2, j] = new
+        hat, _ = norm_rows(new)
+        a_all[l + 1, j, my_c] = (hat * vec(l + 1, 0) + vec(l + 1, 1)).astype(BF16)
+        own_copy(a_all.at[l + 1], j).start()
+
+    def last_send(slot, j):
+        send_partial(slot, dot_nt(z_all[LAYERS - 1, j], wt[LAYERS - 1, 2].reshape(D, D)))
+
+    def last_end(slot, j):
+        last = res.at[2 * LAYERS - 1]
+        last[j] = last[j] + total(slot, 2) + vec(LAYERS - 1, 5)
+        near_copy(last, bo_hbm, 0, j).start()
+        far_copy(last, bo_hbm, 0, j).start()
 
     def when_chunk(tick, offset, func):
         @pl.when(jnp.logical_and(tick >= offset, tick < offset + CHUNKS))
@@ -955,7 +957,7 @@
         send_partial(j, dot_nt(du_all[j], wt[l, 1].reshape(D, D)))
 
     def middle_back(l, j):
-        grad = total(j, 0)
+        grad = total(j, 1)
         d_rows, d_gain, d_shift = norm_back(grad, res[2 * l + 1, j], vec(l, 2))
         y_rows = y_own[j]
         add_vec(l, 5, jnp.sum(y_rows, axis=0, keepdims=True))
@@ -1014,7 +1016,7 @@
         send_partial(j, dot_nt(dx_mat, wt[l, 0].reshape(D, D)[:, 0:640]))
 
     def layer_begin(l, j):
-        grad = total(j, 1)
+        grad = total(j, 0)
         d_rows, d_gain, d_shift = norm_back(grad, res[2 * l, j], vec(l, 0))
         add_vec(l, 0, d_gain)
         add_vec(l, 1, d_shift)
@@ -1210,9 +1212,6 @@
         a_all[0, j, other_c] = (hat * vec(0, 0) + vec(0, 1)).astype(BF16)
         return carry
 
-    def y_copy(j):
-        return remote(y_all.at[j, my_c], y_all.at[j, my_c], y_s.at[j], y_r.at[j], sibling)
-
     def first_grad(j, carry):
         load_cot(j).wait()
         rows = jnp.where(kid_col[2 * j + my_c][:, 0:1] >= 0.0, y_own[j], 0.0)
@@ -1253,22 +1252,17 @@
             when_chunk(tick, 1, lambda j: pass_on(j, 0))
             when_chunk(tick, 5, lambda j: pass_on(j, 1))
 
-            @pl.when(l == LAYERS - 1)
+            when_chunk(tick, 3, lambda j: middle(l, j))
+
+            @pl.when(l < LAYERS - 1)
             def _():
-                when_chunk(tick, 9, lambda j: pass_on(j, 0))
-
-            when_chunk(tick, 3, lambda j: middle(l, j))
-            when_chunk(tick, 7, lambda j: layer_end(l, j))
+                when_chunk(tick, 7, lambda j: layer_end(0, j))
+
             when_chunk(tick, 0, lambda j: attend_chunk(l, j))
 
             def next_project(j):
                 own_copy(a_all.at[LAYERS - 1], j).wait()
                 project(LAYERS - 1, j)
-
-            def first_back(j):
-                far_copy(x_out, bo_hbm, 0, j).wait_recv()
-                y_copy(j).wait()
-                mlp_back(LAYERS - 1, j)
 
             @pl.when(l == 0)
             def _():
@@ -1326,17 +1320,15 @@
             def _():
                 when_chunk(tick, 8, next_project)
 
-            @pl.when(l == LAYERS - 1)
-            def _():
-                at(tick == 7, lambda: prepare_back(LAYERS - 1))
-                when_chunk(tick, 8, first_back)
-
+            at(jnp.logical_and(l == LAYERS - 1, tick == 8), lambda: prepare_back(LAYERS - 1))
             return inner
 
-        lax.fori_loop(0, 13, step, 0)
+        lax.fori_loop(0, 12, step, 0)
         return carry
 
     lax.fori_loop(0, LAYERS, forward_layer, 0)
+    for step in range(1, n_dp):
+        msg_copy(step).wait_send()
 
     def finish_part(l, p):
         scatter_end(l, p)
@@ -1353,6 +1345,14 @@
             scatter_middle(LAYERS - 1, 0)
 
         def step(tick, inner):
+            at(tick == 1, lambda: last_send(0, 2 * n))
+
+            @pl.when(tick == 2)
+            def _():
+                last_send(1, 2 * n + 1)
+                pass_on(0, 2)
+
+            at(tick == 3, lambda: pass_on(1, 2))
             middle_back(l, tick)
             at(tick == 0, lambda: up_grad(l))
 
@@ -1363,13 +1363,14 @@
         lax.fori_loop(0, CHUNKS, step, 0)
 
         def step_two(tick, inner):
-            when_chunk(tick, 1, lambda j: pass_on(j, 1))
+            when_chunk(tick, 1, lambda j: pass_on(j, 0))
 
             @pl.when(upper)
             def _():
-                when_chunk(tick, 6, lambda j: pass_on(j, 0))
+                when_chunk(tick, 6, lambda j: pass_on(j, 1))
 
             when_chunk(tick, 4, lambda j: layer_begin(l, j))
+            at(tick < 2, lambda: last_end(tick, 2 * n + tick))
             when_chunk(tick, 0, lambda j: project_back(l, j))
             at(tick == 3, lambda: qkv_grad(l))
 
@@ -1413,23 +1414,23 @@
     def gmsg_copy(step):
         dest = lax.rem(me + step, n_dp)
         return remote(
-            gmsg_out.at[dest], gmsg_in.at[me], gm_s.at[step - 1], gm_r.at[me], dp_dev(dest)
+            gmsg_out.at[dest], msg_in.at[me], gm_s.at[step - 1], gm_r.at[me], dp_dev(dest)
         )
 
     def gmsg_from(step):
         src = lax.rem(me + step, n_dp)
-        return remote(gmsg_out.at[src], gmsg_in.at[src], gm_s.at[step - 1], gm_r.at[src], dp_dev(src))
+        return remote(gmsg_out.at[src], msg_in.at[src], gm_s.at[step - 1], gm_r.at[src], dp_dev(src))
 
     for step in range(1, n_dp):
         gmsg_copy(step).start()
-    gmsg_in[me] = gmsg_out[me]
+    msg_in[me] = gmsg_out[me]
     scatter_middle(0, 0)
     finish_part(0, 1)
     for step in range(1, n_dp):
         gmsg_from(step).wait_recv()
-    summed = gmsg_in[0]
+    summed = msg_in[0]
     for s in range(1, n_dp):
-        summed = summed + gmsg_in[s]
+        summed = summed + msg_in[s]
     sg_ref[...] = summed
 
     scatter_end(0, 0)
@@ -1485,13 +1486,11 @@
     for copy in block_copies(0, 0):
         copy.wait()
     for step in range(1, n_dp):
-        msg_copy(step).wait_send()
         gmsg_copy(step).wait_send()
         nd_copy(step).wait_send()
     for j in range(CHUNKS):
-        if j >= 2:
-            near_copy(x_out, bo_hbm, 0, j).wait()
-            far_copy(x_out, bo_hbm, 0, j).wait_send()
+        near_copy(res.at[2 * LAYERS - 1], bo_hbm, 0, j).wait()
+        far_copy(res.at[2 * LAYERS - 1], bo_hbm, 0, j).wait()
         near_copy(y_own, ig_hbm, 1, j).wait()
         far_copy(y_own, ig_hbm, 1, j).wait()
 
@@ -1530,13 +1529,13 @@
         buf((CHUNKS, 2, HALF, D)),
         buf((CHUNKS, HALF, D)),
         buf((2, CHUNKS, HALF, D)),
+        buf((2, HALF, D)),
         buf((3, D, D)),
         buf((LAYERS, 3, n_z, B, D)),
         buf((LAYERS, 3, n_z - 1, B, D)),
-        buf((8, B, 128), F32),
+        buf((6, B, 128), F32),
         buf((LAYERS * GROUP, 72, 128), F32),
         buf((B, D), F32),
-        buf((2, HALF, D), F32),
         buf((8, HALF, 128), F32),
         buf((CHUNKS, 8, CHUNK), F32),
         buf((LAYERS, 8, D), F32),
@@ -1546,7 +1545,6 @@
         buf((LAYERS, 8, D), F32),
         buf((n_dp, 16, 256), F32),
         buf((n_dp, 16, 256), F32),
-        buf((n_dp, 16, 256), F32),
         buf((2, 8, 128), F32),
         buf((2, 8, 128), F32),
         buf((n_dp, 8, 128), F32),
@@ -1554,8 +1552,8 @@
         dma((LAYERS, 3, n_dp)),
         dma((CHUNKS,)),
         dma((CHUNKS,)),
-        dma((2, CHUNKS)),
-        dma((2, CHUNKS)),
+        dma((3, CHUNKS)),
+        dma((3, CHUNKS)),
         dma((CHUNKS,)),
         dma((CHUNKS,)),
         dma((LAYERS, 3, n_z)),
@@ -1597,7 +1595,7 @@
         out_specs=(hbm, hbm, hbm, hbm, hbm, hbm, vmem, vmem),
         scratch_shapes=scratch,
         compiler_params=pltpu.CompilerParams(
-            collective_id=0, has_side_effects=True, vmem_limit_bytes=60 * 1024 * 1024
+            collective_id=0, has_side_effects=True, vmem_limit_bytes=61 * 1024 * 1024
         ),
         cost_estimate=pl.CostEstimate(
             flops=30_000_000_000, bytes_accessed=30_000_000, transcendentals=20_000_000
@@ -1682,7 +1680,7 @@
 
 
 def update_call(grads, lefts, rights, dirs, weights, left, right, sums, norms, split, shared, outs):
-    per = 6
+    per = GROUP
     count = LAYERS * GROUP
     flat = pl.BlockSpec((per, 72, 128), lambda i: (i, 0, 0))
     rows = pl.BlockSpec((2 * HALF * CHUNKS * per // count, D), lambda i: (i, 0))

time: 266 us -> 249 us (0.936)
  Pallas kernels: 264 us -> 247 us
    pallas_call x1, Pallas kernels: 250 us -> 236 us  [train_call(): pl.pallas_call(functools.partial(train_kernel, n_y), out_shape=(rows_shap...]
    pallas_call x1, Pallas kernels: 14.6 us -> 10.9 us  [update_call(): pl.pallas_call(update_kernel, grid=(count // per,), out_shape=(*[flat_sha...]
where the time goes in v3:
time: 249 us
  Pallas kernels  247 us (99%)
    pallas_call x1, Pallas kernels, train_call(): pl.pallas_call(functools.partial(train_kernel, n_y), out_shape=(rows_shap...  236 us
    pallas_call x1, Pallas kernels, update_call(): pl.pallas_call(update_kernel, grid=(count // per,), out_shape=(*[flat_sha...  10.9 us

profile of v3, /device:TPU:0, one launch (start us, length us, event | category | flops | bytes accessed | tf_op | source)
XLA Modules:
  0.0 248.6 jit_solution(4488756221247937084)
XLA Ops:
  1.3 236.2 %train.1 = (f32[4,2,128,768]{3,2,1,0:T(8,128)}, f32[4,2,128,768]{3,2,1,0:T(8,128)}, f32[2,24,72,128]{3,2,1,0:T(8,128)}, f32[2,24,72,128]{3,2,1,0:T(8,128)}, f32[...) custom-call(f32[4,2,128,768]{3,2,1,0:T(8,128)} %bitcast.37, ...), custom_call_target="tpu_custom_call" | custom-call | flops 30000001024 | bytes 30000000 | tf_op jit(solution)/shard_map/train/pallas_call | solution.py:1585
  237.5 10.9 %update.1 = (f32[48,72,128]{2,1,0:T(8,128)}, f32[48,72,128]{2,1,0:T(8,128)}, f32[48,72,128]{2,1,0:T(8,128)}, f32[48,72,128]{2,1,0:T(8,128)}, f32[2,1,144]{2,1,0:...) custom-call(f32[48,72,128]{2,1,0:T(8,128)} %bitcast.31, ...), custom_call_target="tpu_custom_call" | custom-call | tf_op jit(solution)/shard_map/update/pallas_call | solution.py:1693

commit v4 on v3

--- a/solution.py
+++ b/solution.py
@@ -709,6 +709,7 @@
         def _():
             gather_send(l, p, me, 1, me - n_y).start()
 
+    def own_beside(l, p):
         gather_send(l, p, me, 2, y_peers()[0]).start()
 
     def wave(l, p, hop):
@@ -766,8 +767,14 @@
         load_blocks(l).wait()
         for p in range(3):
             relayout(l, p)
-            if p == 0:
-                at(l == 0, lambda: own_send(0, 0))
+            if p < 2:
+
+                @pl.when(l == 0)
+                def _():
+                    if p == 0:
+                        own_send(0, 0)
+                    own_beside(0, p)
+
         return carry
 
     lax.fori_loop(0, LAYERS, relayout_layer, 0)
@@ -1075,8 +1082,8 @@
         for s in list(range(1, n_z)) + [0]:
             pair_copy(l, p, z_peer(s)).start()
 
-    def scatter_middle(l, p):
-        for s in list(range(1, n_z)) + [0]:
+    def scatter_middle(l, p, steps=(1, 2, 3, 0)):
+        for s in steps:
             z = z_peer(s)
             pair_copy(l, p, z).wait_recv()
             ref = slab(dw, p, z * n_y + my_y)
@@ -1228,15 +1235,17 @@
         copy.start()
     wave(0, 0, 1)
     own_send(0, 1)
+    own_beside(0, 2)
     lax.fori_loop(0, CHUNKS // 2, first_norm, 0)
     wave(0, 0, 2)
     lax.fori_loop(CHUNKS // 2, CHUNKS, first_norm, 0)
     wave(0, 0, 3)
     wave(0, 1, 1)
     lax.fori_loop(0, CHUNKS, first_grad, 0)
+    own_send(0, 2)
     gather_finish(0, 0)
     wave(0, 1, 2)
-    own_send(0, 2)
+    own_beside(1, 0)
     lax.fori_loop(0, CHUNKS, first_project, 0)
 
     def prepare_back(l):
@@ -1258,12 +1267,6 @@
             def _():
                 when_chunk(tick, 7, lambda j: layer_end(0, j))
 
-            when_chunk(tick, 0, lambda j: attend_chunk(l, j))
-
-            def next_project(j):
-                own_copy(a_all.at[LAYERS - 1], j).wait()
-                project(LAYERS - 1, j)
-
             @pl.when(l == 0)
             def _():
                 @pl.when(tick == 1)
@@ -1271,10 +1274,11 @@
                     wave(0, 1, 3)
                     wave(0, 2, 1)
 
-                @pl.when(tick == 3)
+                @pl.when(tick == 2)
                 def _():
                     wave(0, 2, 2)
                     own_send(1, 0)
+                    own_beside(1, 1)
 
                 @pl.when(tick == 4)
                 def _():
@@ -1286,33 +1290,47 @@
                 def _():
                     wave(1, 0, 2)
                     own_send(1, 1)
-
-                @pl.when(tick == 7)
+                    own_beside(1, 2)
+
+                @pl.when(tick == 6)
                 def _():
                     wave(1, 0, 3)
                     wave(1, 1, 1)
 
-                at(tick == 8, lambda: gather_finish(1, 0))
-
-                @pl.when(tick == 9)
+                @pl.when(tick == 7)
                 def _():
                     wave(1, 1, 2)
                     own_send(1, 2)
 
-                @pl.when(tick == 11)
+                @pl.when(tick == 8)
+                def _():
+                    gather_finish(1, 0)
+
+                @pl.when(tick == 9)
                 def _():
                     wave(1, 1, 3)
                     wave(1, 2, 1)
 
+                @pl.when(tick == 10)
+                def _():
+                    wave(1, 2, 2)
+
+                @pl.when(tick == 11)
+                def _():
+                    wave(1, 2, 3)
+
             @pl.when(l == 1)
             def _():
-                at(tick == 0, lambda: wave(1, 2, 2))
-                at(tick == 1, lambda: wave(1, 2, 3))
-
                 @pl.when(tick == 4)
                 def _():
                     gather_finish(1, 1)
                     gather_finish(1, 2)
+
+            when_chunk(tick, 0, lambda j: attend_chunk(l, j))
+
+            def next_project(j):
+                own_copy(a_all.at[LAYERS - 1], j).wait()
+                project(LAYERS - 1, j)
 
             when_chunk(tick, 4, lambda j: mlp(l, j))
 
@@ -1354,7 +1372,7 @@
 
             at(tick == 3, lambda: pass_on(1, 2))
             middle_back(l, tick)
-            at(tick == 0, lambda: up_grad(l))
+            at(tick == 2, lambda: up_grad(l))
 
             at(tick == 3, lambda: scatter_middle(l, 2))
             attend_back(l, tick)
@@ -1376,8 +1394,14 @@
 
             @pl.when(lower)
             def _():
-                at(tick == 4, lambda: finish_part(LAYERS - 1, 1))
-                at(tick == 5, lambda: finish_part(LAYERS - 1, 0))
+                @pl.when(tick == 4)
+                def _():
+                    scatter_middle(0, 1)
+                    finish_part(LAYERS - 1, 1)
+
+                at(tick == 5, lambda: scatter_middle(0, 0, (1,)))
+                at(tick == 6, lambda: scatter_middle(0, 0, (2,)))
+                at(tick == 7, lambda: scatter_middle(0, 0, (3,)))
 
             def next_back(j):
                 own_copy(y_all, j).wait()
@@ -1388,8 +1412,11 @@
                 at(tick == 4, lambda: prepare_back(l - 1))
                 when_chunk(tick, 5, next_back)
 
-            at(tick == 5, lambda: scatter_middle(l, 1))
-            at(tick == 6, lambda: finish_part(l, 2))
+            @pl.when(upper)
+            def _():
+                at(tick == 5, lambda: scatter_middle(l, 1))
+                at(tick == 6, lambda: finish_part(l, 2))
+
             return inner
 
         lax.fori_loop(0, 10, step_two, 0)
@@ -1424,7 +1451,9 @@
     for step in range(1, n_dp):
         gmsg_copy(step).start()
     msg_in[me] = gmsg_out[me]
-    scatter_middle(0, 0)
+    scatter_middle(0, 0, (0,))
+    finish_part(LAYERS - 1, 0)
+    finish_part(0, 2)
     finish_part(0, 1)
     for step in range(1, n_dp):
         gmsg_from(step).wait_recv()
@@ -1453,11 +1482,7 @@
         nb_out[hop] = jnp.broadcast_to(packed, (8, 128))
         swap = remote(nb_out.at[hop], nb_in.at[hop], nb_s.at[hop], nb_r.at[hop], dev)
         swap.start()
-        if hop == 0:
-            swap.wait()
-        else:
-            block_update(0, 0)
-            swap.wait()
+        swap.wait()
         packed = packed + nb_in[hop, 0:1, :]
     row8 = lax.broadcasted_iota(jnp.int32, (8, 128), 0)
     nd_in[me] = jnp.where(row8 == 0, packed, jnp.where(row8 == 1, shared_sums, 0.0))
@@ -1472,6 +1497,7 @@
 
     for step in range(1, n_dp):
         nd_copy(step).start()
+    block_update(0, 0)
     for step in range(1, n_dp):
         nd_from(step).wait_recv()
     acc = nd_in[0]

time: 249 us -> 242 us (0.972)
  Pallas kernels: 247 us -> 240 us
    pallas_call x1, Pallas kernels: 236 us -> 230 us  [train_call(): pl.pallas_call(functools.partial(train_kernel, n_y), out_shape=(rows_shap...]
where the time goes in v4:
time: 242 us
  Pallas kernels  240 us (99%)
    pallas_call x1, Pallas kernels, train_call(): pl.pallas_call(functools.partial(train_kernel, n_y), out_shape=(rows_shap...  230 us
    pallas_call x1, Pallas kernels, update_call(): pl.pallas_call(update_kernel, grid=(count // per,), out_shape=(*[flat_sha...  10.9 us

profile of v4, /device:TPU:0, one launch (start us, length us, event | category | flops | bytes accessed | tf_op | source)
XLA Modules:
  0.0 242.0 jit_solution(11986292964918696708)
XLA Ops:
  1.3 229.6 %train.1 = (f32[4,2,128,768]{3,2,1,0:T(8,128)}, f32[4,2,128,768]{3,2,1,0:T(8,128)}, f32[2,24,72,128]{3,2,1,0:T(8,128)}, f32[2,24,72,128]{3,2,1,0:T(8,128)}, f32[...) custom-call(f32[4,2,128,768]{3,2,1,0:T(8,128)} %bitcast.37, ...), custom_call_target="tpu_custom_call" | custom-call | flops 30000001024 | bytes 30000000 | tf_op jit(solution)/shard_map/train/pallas_call | solution.py:1611
  230.9 10.9 %update.1 = (f32[48,72,128]{2,1,0:T(8,128)}, f32[48,72,128]{2,1,0:T(8,128)}, f32[48,72,128]{2,1,0:T(8,128)}, f32[48,72,128]{2,1,0:T(8,128)}, f32[2,1,144]{2,1,0:...) custom-call(f32[48,72,128]{2,1,0:T(8,128)} %bitcast.31, ...), custom_call_target="tpu_custom_call" | custom-call | tf_op jit(solution)/shard_map/update/pallas_call | solution.py:1719

commit v5 on v4

--- a/solution.py
+++ b/solution.py
@@ -1269,9 +1269,12 @@
 
             @pl.when(l == 0)
             def _():
+                @pl.when(tick == 0)
+                def _():
+                    wave(0, 1, 3)
+
                 @pl.when(tick == 1)
                 def _():
-                    wave(0, 1, 3)
                     wave(0, 2, 1)
 
                 @pl.when(tick == 2)
@@ -1280,10 +1283,13 @@
                     own_send(1, 0)
                     own_beside(1, 1)
 
+                @pl.when(tick == 3)
+                def _():
+                    wave(0, 2, 3)
+
                 @pl.when(tick == 4)
                 def _():
                     gather_finish(0, 1)
-                    wave(0, 2, 3)
                     wave(1, 0, 1)
 
                 @pl.when(tick == 5)
@@ -1305,17 +1311,14 @@
                 @pl.when(tick == 8)
                 def _():
                     gather_finish(1, 0)
+                    wave(1, 1, 3)
+                    wave(1, 2, 1)
 
                 @pl.when(tick == 9)
                 def _():
-                    wave(1, 1, 3)
-                    wave(1, 2, 1)
+                    wave(1, 2, 2)
 
                 @pl.when(tick == 10)
-                def _():
-                    wave(1, 2, 2)
-
-                @pl.when(tick == 11)
                 def _():
                     wave(1, 2, 3)
 
@@ -1363,14 +1366,17 @@
             scatter_middle(LAYERS - 1, 0)
 
         def step(tick, inner):
-            at(tick == 1, lambda: last_send(0, 2 * n))
-
-            @pl.when(tick == 2)
+            @pl.when(upper)
             def _():
-                last_send(1, 2 * n + 1)
-                pass_on(0, 2)
-
-            at(tick == 3, lambda: pass_on(1, 2))
+                at(tick == 1, lambda: last_send(0, 0))
+
+                @pl.when(tick == 2)
+                def _():
+                    last_send(1, 1)
+                    pass_on(0, 2)
+
+                at(tick == 3, lambda: pass_on(1, 2))
+
             middle_back(l, tick)
             at(tick == 2, lambda: up_grad(l))
 
@@ -1388,12 +1394,25 @@
                 when_chunk(tick, 6, lambda j: pass_on(j, 1))
 
             when_chunk(tick, 4, lambda j: layer_begin(l, j))
-            at(tick < 2, lambda: last_end(tick, 2 * n + tick))
+            at(jnp.logical_and(upper, tick < 2), lambda: last_end(tick, tick))
             when_chunk(tick, 0, lambda j: project_back(l, j))
             at(tick == 3, lambda: qkv_grad(l))
 
             @pl.when(lower)
             def _():
+                @pl.when(tick == 5)
+                def _():
+                    far_copy(y_own, ig_hbm, 1, 0).wait_recv()
+                    last_send(0, 2)
+
+                @pl.when(tick == 6)
+                def _():
+                    pass_on(0, 2)
+                    far_copy(y_own, ig_hbm, 1, 1).wait_recv()
+                    last_send(1, 3)
+
+                at(tick == 7, lambda: pass_on(1, 2))
+
                 @pl.when(tick == 4)
                 def _():
                     scatter_middle(0, 1)
@@ -1497,6 +1516,8 @@
 
     for step in range(1, n_dp):
         nd_copy(step).start()
+    last_end(0, 2)
+    last_end(1, 3)
     block_update(0, 0)
     for step in range(1, n_dp):
         nd_from(step).wait_recv()
@@ -1518,7 +1539,10 @@
         near_copy(res.at[2 * LAYERS - 1], bo_hbm, 0, j).wait()
         far_copy(res.at[2 * LAYERS - 1], bo_hbm, 0, j).wait()
         near_copy(y_own, ig_hbm, 1, j).wait()
-        far_copy(y_own, ig_hbm, 1, j).wait()
+        if j < 2:
+            far_copy(y_own, ig_hbm, 1, j).wait_send()
+        else:
+            far_copy(y_own, ig_hbm, 1, j).wait()
 
 
 def train_call(n_y, x_rows, ct_rows, seg, long_flag, blocks, left, right, split, shared):

time: 242 us -> 240 us (level)
    pallas_call x1, Pallas kernels: 230 us -> 227 us  [train_call(): pl.pallas_call(functools.partial(train_kernel, n_y), out_shape=(rows_shap...]
where the time goes in v5:
time: 240 us
  Pallas kernels  238 us (99%)
    pallas_call x1, Pallas kernels, train_call(): pl.pallas_call(functools.partial(train_kernel, n_y), out_shape=(rows_shap...  227 us
    pallas_call x1, Pallas kernels, update_call(): pl.pallas_call(update_kernel, grid=(count // per,), out_shape=(*[flat_sha...  10.9 us

profile of v5, /device:TPU:0, one launch (start us, length us, event | category | flops | bytes accessed | tf_op | source)
XLA Modules:
  0.0 239.5 jit_solution(9835978014170150742)
XLA Ops:
  1.3 227.2 %train.1 = (f32[4,2,128,768]{3,2,1,0:T(8,128)}, f32[4,2,128,768]{3,2,1,0:T(8,128)}, f32[2,24,72,128]{3,2,1,0:T(8,128)}, f32[2,24,72,128]{3,2,1,0:T(8,128)}, f32[...) custom-call(f32[4,2,128,768]{3,2,1,0:T(8,128)} %bitcast.37, ...), custom_call_target="tpu_custom_call" | custom-call | flops 30000001024 | bytes 30000000 | tf_op jit(solution)/shard_map/train/pallas_call | solution.py:1635
  228.5 10.9 %update.1 = (f32[48,72,128]{2,1,0:T(8,128)}, f32[48,72,128]{2,1,0:T(8,128)}, f32[48,72,128]{2,1,0:T(8,128)}, f32[48,72,128]{2,1,0:T(8,128)}, f32[2,1,144]{2,1,0:...) custom-call(f32[48,72,128]{2,1,0:T(8,128)} %bitcast.31, ...), custom_call_target="tpu_custom_call" | custom-call | tf_op jit(solution)/shard_map/update/pallas_call | solution.py:1743

commit v6 on v5

--- a/solution.py
+++ b/solution.py
@@ -1433,7 +1433,7 @@
 
             @pl.when(upper)
             def _():
-                at(tick == 5, lambda: scatter_middle(l, 1))
+                at(tick == 4, lambda: scatter_middle(l, 1))
                 at(tick == 6, lambda: finish_part(l, 2))
 
             return inner

time: 240 us -> 240 us (level)
  no operation moved by 1% of the time
where the time goes in v6:
time: 240 us; the launch traced here: 239 us
  Pallas kernels  238 us (99%)
    pallas_call x1, Pallas kernels, train_call(): pl.pallas_call(functools.partial(train_kernel, n_y), out_shape=(rows_shap...  227 us
    pallas_call x1, Pallas kernels, update_call(): pl.pallas_call(update_kernel, grid=(count // per,), out_shape=(*[flat_sha...  10.9 us

profile of v6, /device:TPU:0, one launch (start us, length us, event | category | flops | bytes accessed | tf_op | source)
XLA Modules:
  0.0 239.5 jit_solution(6633922488102790318)
XLA Ops:
  1.3 227.1 %train.1 = (f32[4,2,128,768]{3,2,1,0:T(8,128)}, f32[4,2,128,768]{3,2,1,0:T(8,128)}, f32[2,24,72,128]{3,2,1,0:T(8,128)}, f32[2,24,72,128]{3,2,1,0:T(8,128)}, f32[...) custom-call(f32[4,2,128,768]{3,2,1,0:T(8,128)} %bitcast.37, ...), custom_call_target="tpu_custom_call" | custom-call | flops 30000001024 | bytes 30000000 | tf_op jit(solution)/shard_map/train/pallas_call | solution.py:1635
  228.4 10.9 %update.1 = (f32[48,72,128]{2,1,0:T(8,128)}, f32[48,72,128]{2,1,0:T(8,128)}, f32[48,72,128]{2,1,0:T(8,128)}, f32[48,72,128]{2,1,0:T(8,128)}, f32[2,1,144]{2,1,0:...) custom-call(f32[48,72,128]{2,1,0:T(8,128)} %bitcast.31, ...), custom_call_target="tpu_custom_call" | custom-call | tf_op jit(solution)/shard_map/update/pallas_call | solution.py:1743
